TPU v7x, 512 devices: a whole 4x4x16 slice. The times are simulated.
512 devices in a mesh: row: 32 (over x, z_lo, core), col: 16 (over z_hi, y).
Axes of the slice: x: 4, y: 4, z: 16 (z_hi: 4, z_lo: 4; z = z_hi * 4 + z_lo), core: 2. Of those that a mesh axis runs over, the one named last changes fastest.
Arguments:
- initial_block: float32 [64, 32768], P(None, ('row', 'col')), may hold values from -6 to 6
- matrix_tiles: float32 [32, 16, 4, 128, 128], P('row', 'col'), may hold values from -0.0625 to 0.0625
- tile_rows: int32 [32, 16, 4], P('row', 'col'), may hold values from 0 to 7
- tile_columns: int32 [32, 16, 4], P('row', 'col'), may hold values from 0 to 15
Outputs:
- basis: float32 [64, 32768], P(None, ('row', 'col'))
- rayleigh: float32 [64, 64], replicated
- residual: float32 [64, 32768], P(None, ('row', 'col'))
All inputs are finite; a program needn't handle non-finite values.
Results may differ from a plain program's by a relative error of at most 0.00018.
Values sent between devices are 32-bit elements; how exact they have to be, the bound alone decides.
No kernel may reach another device: no remote copies, remote signals or barrier semaphores. Data moves between devices by JAX's collectives and lax.ppermute only.
A program may use at most 64 MiB of HBM per device.

v0:
```python
import functools

import jax
import jax.numpy as jnp
from jax import lax
from jax.experimental import pallas as pl
from jax.experimental.pallas import tpu as pltpu
from jax.sharding import Mesh
from jax.sharding import PartitionSpec as P

TILE = 128
HALF = 64
VEC = 64
GROUP = 8
PIECES = 4
GIVEN = (1, 3, 4, 4)
STORED = (3, 4, 4, 0)
ITERS = 4
STEP = 0.5
MOMENTUM = 0.4
AXES = ("x", "zl", "core", "zh", "y")
ROW = ("x", "zl", "core")
CHIPS = ("x", "zl")
COL = ("zh", "y")
SPLIT = (4, 4, 2, 4, 4)


def dot(a, b, contract=((1,), (0,))):
    return lax.dot_general(
        a,
        b,
        (contract, ((), ())),
        precision=lax.Precision.HIGHEST,
        preferred_element_type=jnp.float32,
    )


NT = ((1,), (1,))


def lanes(rows):
    return lax.broadcasted_iota(jnp.int32, (rows, TILE), 1)


def swap_halves(v):
    return pltpu.roll(v, HALF, 1)


def pack_pair(tile):
    low = lanes(VEC // 2) < HALF
    top, bottom = tile[: VEC // 2], tile[VEC // 2 :]
    even = jnp.where(low, top, swap_halves(bottom))
    odd = jnp.where(low, swap_halves(top), bottom)
    return even, odd


def unpack_pair(even, odd):
    low = lanes(VEC // 2) < HALF
    top = jnp.where(low, even, swap_halves(odd))
    bottom = jnp.where(low, swap_halves(even), odd)
    return top, bottom


def inverse_cholesky(packed):
    low = lanes(VEC // 2) < HALF
    row_id = lax.broadcasted_iota(jnp.int32, (VEC // 2, TILE), 0)
    col_id = lanes(VEC // 2)
    eye_top = jnp.where(col_id - HALF == row_id, 1.0, 0.0)
    eye_bottom = jnp.where(col_id - HALF == row_id + VEC // 2, 1.0, 0.0)
    top = jnp.where(low, packed, eye_top)
    bottom = jnp.where(low, swap_halves(packed), eye_bottom)
    count = VEC // GROUP
    groups = [half[GROUP * g : GROUP * (g + 1)] for half in (top, bottom) for g in range(count // 2)]
    sub = lax.broadcasted_iota(jnp.int32, (GROUP, TILE), 0)
    lane = lanes(GROUP)

    def wide(v):
        return jnp.broadcast_to(v, (GROUP, TILE))

    out = []
    for own in range(count):
        first = own * GROUP
        columns = {
            g: [wide(groups[g][:, first + k : first + k + 1]) for k in range(GROUP)] for g in range(own, count)
        }
        rows = [wide(groups[own][k : k + 1, :]) for k in range(GROUP)]
        corner = [
            [wide(columns[own][m][k : k + 1, :]) if m >= k else None for m in range(GROUP)] for k in range(GROUP)
        ]
        scales = []
        for k in range(GROUP):
            scale = 1.0 / corner[k][k]
            scales.append(scale)
            for l in range(k + 1, GROUP):
                factor = corner[k][l] * scale
                rows[l] = rows[l] - factor * rows[k]
                for m in range(l, GROUP):
                    corner[l][m] = corner[l][m] - factor * corner[k][m]
        for g in range(own + 1, count):
            column = columns[g]
            for k in range(GROUP):
                factor = column[k] * scales[k]
                groups[g] = groups[g] - factor * rows[k]
                for m in range(k + 1, GROUP):
                    column[m] = column[m] - factor * corner[k][m]
        block, diagonal = rows[0], corner[0][0]
        for k in range(1, GROUP):
            block = jnp.where(sub == k, rows[k], block)
            diagonal = jnp.where(sub == k, corner[k][k], diagonal)
        out.append(jnp.where(lane >= HALF, block / jnp.sqrt(diagonal), 0.0))
    return jnp.concatenate(out, axis=0)


def unpack_square(packed):
    return jnp.concatenate([packed, swap_halves(packed)], axis=0)[:, :HALF]


def small_algebra(recv_ref, at, n_y):
    gram, projected = sum_squares(recv_ref, at, n_y)
    projected = unpack_square(projected)
    right = inverse_cholesky(gram)
    left = swap_halves(right)
    inverse = left[:, :HALF]
    rayleigh = dot(dot(inverse, projected), inverse, NT)
    mixed = right - dot(rayleigh, left)
    return left, right, mixed, rayleigh


def sum_squares(recv_ref, at, n_y):
    each = VEC // 2 // n_y
    sums = []
    for which in range(2):
        starts = [at + (2 * y + which) * each for y in range(n_y)]
        sums.append(jnp.concatenate([recv_ref[0, i : i + each, :] + recv_ref[1, i : i + each, :] for i in starts], axis=0))
    return sums


def emit_products(
    n_row, n_col, q, factor, own_gram, tiles_ref, where_ref, rows_ref, cols_ref, keep_ref, give_ref, send_y_ref,
    direct, mirrored,
):
    row_tiles, col_tiles = n_col // 2, n_row // 2
    direct[...] = jnp.zeros_like(direct)
    mirrored[...] = jnp.zeros_like(mirrored)
    cross = jnp.zeros((VEC, VEC), jnp.float32)
    for t in range(tiles_ref.shape[0]):
        i, j = rows_ref[t], cols_ref[t]
        tile = tiles_ref[t]
        row_pick = q[i]
        column_pick = q[row_tiles + j]
        product = dot(column_pick, tile, NT)
        direct[i] += product
        mirrored[j] += dot(row_pick, tile)
        cross = cross + dot(product, row_pick, NT)
    gram, projected = own_gram()
    projected = projected + factor * (cross + cross.T)
    low = lanes(VEC // 2) < HALF

    def pack_square(m):
        wide = jnp.concatenate([m, m], axis=1)
        return jnp.where(low, wide[: VEC // 2], wide[VEC // 2 :])

    n_y = send_y_ref.shape[0]
    each = VEC // 2 // n_y
    at = send_y_ref.shape[1] - 2 * each
    for which, square in enumerate((pack_square(gram), pack_square(projected))):
        for y in range(n_y):
            start = at + which * each
            send_y_ref[y, start : start + each, :] = square[y * each : (y + 1) * each]
    second = where_ref[2] == 1
    for b in range(col_tiles):
        even, odd = pack_pair(mirrored[b])
        keep_ref[b] = jnp.where(second, odd, even)
        give_ref[b] = jnp.where(second, even, odd)
    for s in range(row_tiles):
        for c, block in zip((2 * s, 2 * s + 1), pack_pair(direct[s])):
            zh, y = c // n_y, c % n_y
            send_y_ref[y, zh * (VEC // 2) : (zh + 1) * (VEC // 2), :] = block


def unpack_gathered(recv_row_ref, recv_col_ref, n_row, n_col, out):
    n_y = recv_col_ref.shape[0]
    half = VEC // 2

    def col_block(c):
        zh, y = c // n_y, c % n_y
        return recv_col_ref[y, zh * half : (zh + 1) * half, :]

    for s in range(n_col // 2):
        top, bottom = unpack_pair(col_block(2 * s), col_block(2 * s + 1))
        out[s, :half, :] = top
        out[s, half:, :] = bottom
    for b in range(n_row // 2):
        top, bottom = unpack_pair(*(recv_row_ref[core, b * half : (b + 1) * half, :] for core in range(2)))
        out[n_col // 2 + b, :half, :] = top
        out[n_col // 2 + b, half:, :] = bottom


def own_mask(where_ref):
    return (lanes(VEC) // HALF) == where_ref[1]


def first_kernel(
    n_row, n_col, where_ref, rows_ref, cols_ref, tiles_ref, recv_row_ref, recv_col_ref,
    trial_ref, keep_ref, give_ref, send_y_ref, fresh, direct, mirrored, sem,
):
    unpack_gathered(recv_row_ref, recv_col_ref, n_row, n_col, fresh)
    store = pltpu.make_async_copy(fresh, trial_ref, sem)
    store.start()

    def own_gram():
        mine = fresh[where_ref[0]]
        return dot(jnp.where(own_mask(where_ref), mine, 0.0), mine, NT), jnp.zeros((VEC, VEC), jnp.float32)

    emit_products(
        n_row, n_col, fresh, 1.0, own_gram, tiles_ref, where_ref, rows_ref, cols_ref, keep_ref, give_ref, send_y_ref,
        direct, mirrored,
    )
    store.wait()


def middle_kernel(step, n_row, n_col, *refs):
    first, last = step == 0, step == ITERS - 1
    given, stored = GIVEN[step], STORED[step]
    where_ref, rows_ref, cols_ref, tiles_ref, recv_row_ref, recv_col_ref = refs[:6]
    old_refs, refs = refs[6 : 6 + given], refs[6 + given :]
    new_refs, refs = refs[: stored or 2], refs[stored or 2 :]
    keep_ref, give_ref, send_y_ref, state, fresh, direct, mirrored, load_sems, store_sems = refs
    n_tiles = n_col // 2 + n_row // 2
    piece = n_tiles // PIECES

    def moves(outside, sems, count, inward):
        result = []
        for p in range(PIECES):
            tiles = pl.ds(p * piece, piece)
            pairs = [(outside[k].at[tiles], state.at[k, tiles]) for k in range(count)]
            result.append(
                [
                    pltpu.make_async_copy(*(pair if inward else pair[::-1]), sems.at[k, p])
                    for k, pair in enumerate(pairs)
                ]
            )
        return result

    loads = moves(old_refs, load_sems, given, True)
    stores = moves(new_refs, store_sems, stored, False)
    for part in loads:
        for load in part:
            load.start()
    trials, knowns, searches, search_images = (state.at[k] for k in range(4))
    unpack_gathered(recv_row_ref, recv_col_ref, n_row, n_col, fresh)
    left, right, mixed, _ = small_algebra(recv_row_ref, n_row // 2 * (VEC // 2), recv_col_ref.shape[0])
    coefficients = jnp.concatenate([left, right, mixed], axis=0)
    for t in range(n_tiles):
        if t % piece == 0:
            for load in loads[t // piece]:
                load.wait()
        image = fresh[t]
        trial = trials[t]
        trial_image = image if first else knowns[t] - STEP * image
        both = jnp.concatenate([trial, trial_image], axis=0)
        mixtures = dot(coefficients, both)
        basis, new_image, residual = (mixtures[VEC * k : VEC * (k + 1)] for k in range(3))
        fresh[t] = residual
        search = -STEP * residual
        if not first:
            search = search + MOMENTUM * searches[t]
            search_image = -STEP * image
            if given == 4:
                search_image = search_image + MOMENTUM * search_images[t]
            new_image = new_image + MOMENTUM * search_image
            if stored == 4:
                search_images[t] = search_image
        trials[t] = basis + search
        knowns[t] = new_image
        if not last:
            searches[t] = search
        if t % piece == piece - 1:
            for store in stores[t // piece]:
                store.start()
    if last:
        new_refs[0][...] = trials[where_ref[0]]
        new_refs[1][...] = knowns[where_ref[0]]

    def own_gram():
        at = where_ref[0]
        mask = own_mask(where_ref)
        trial = jnp.where(mask, trials[at], 0.0)
        known = jnp.where(mask, knowns[at], 0.0)
        gram = dot(trial, trial, NT)
        projected = dot(trial, known, NT) - STEP * dot(known, fresh[at], NT)
        return gram, projected

    emit_products(
        n_row, n_col, fresh, STEP * STEP, own_gram, tiles_ref, where_ref, rows_ref, cols_ref, keep_ref, give_ref,
        send_y_ref, direct, mirrored,
    )
    for part in stores:
        for store in part:
            store.wait()


def last_kernel(n_y, where_ref, recv_ref, local_ref, trial_ref, known_ref, basis_ref, rayleigh_ref, residual_ref):
    left, right, mixed, rayleigh = small_algebra(recv_ref, 0, n_y)
    block = local_ref[...]
    image = jnp.concatenate(unpack_pair(block, block), axis=0)
    trial = trial_ref[...]
    trial_image = known_ref[...] - STEP * image
    both = jnp.concatenate([trial, trial_image], axis=0)
    odd = where_ref[1] == 1
    basis = dot(left, both)
    residual = dot(mixed, both)
    basis_ref[...] = jnp.where(odd, swap_halves(basis), basis)[:, :HALF]
    residual_ref[...] = jnp.where(odd, swap_halves(residual), residual)[:, :HALF]
    rayleigh_ref[...] = rayleigh


def per_device(split, initial_block, matrix_tiles, tile_rows, tile_columns):
    n_x, n_zl, n_core, n_zh, n_y = split
    n_row, n_col = n_x * n_zl * n_core, n_zh * n_y
    n_tiles = n_row // 2 + n_col // 2
    half = VEC // 2
    sums_rows = 2 * (half // n_y)
    n_direct = n_zh * half
    tiles = matrix_tiles[0, 0]
    rows, cols = tile_rows[0, 0], tile_columns[0, 0]
    my_col = lax.axis_index("zh") * n_y + lax.axis_index("y")
    where = jnp.stack([my_col // 2, my_col % 2, lax.axis_index("core")]).astype(jnp.int32)

    smem = pl.BlockSpec(memory_space=pltpu.SMEM)
    vmem = pl.BlockSpec(memory_space=pltpu.VMEM)
    f32 = jnp.float32
    state = pltpu.HBM((n_tiles, VEC, TILE), f32)
    hbm = pl.BlockSpec(memory_space=pltpu.HBM)
    half_row = jax.ShapeDtypeStruct((n_row // 2, half, TILE), f32)
    send_y = jax.ShapeDtypeStruct((n_y, n_direct + sums_rows, TILE), f32)
    sends = (half_row, half_row, send_y)
    params = pltpu.CompilerParams(vmem_limit_bytes=20 * 1024 * 1024)
    gathered = pltpu.VMEM((n_tiles, VEC, TILE), f32)
    partial_sums = [pltpu.VMEM((n_col // 2, VEC, TILE), f32), pltpu.VMEM((n_row // 2, VEC, TILE), f32)]
    own_tile = jax.ShapeDtypeStruct((VEC, TILE), f32)

    def exchange(blocks, axes):
        return lax.all_to_all(blocks, axes, 0, 0, tiled=True)

    def spread(block, axes, count):
        return exchange(jnp.broadcast_to(block[None], (count,) + block.shape), axes)

    def reduce_row_and_y(keep, give, y_blocks):
        both_cores = keep + lax.ppermute(give, "core", [(0, 1), (1, 0)])
        from_y, both_cores = lax.optimization_barrier((exchange(y_blocks, "y"), both_cores))
        along_y = jnp.sum(from_y, axis=0)
        sums = jnp.broadcast_to(along_y[None, n_direct:], (n_row // 2, sums_rows, TILE))
        mirrored = jnp.sum(exchange(jnp.concatenate([both_cores, sums], axis=1), CHIPS), axis=0)
        return mirrored, along_y[:n_direct]

    def gather_chips(block):
        return spread(block, CHIPS, n_row // 2).reshape(n_row // 2 * half, TILE)

    def apply_and_gather(keep, give, y_blocks):
        mirrored, along_y = reduce_row_and_y(keep, give, y_blocks)
        heard = spread(jnp.concatenate([along_y, mirrored], axis=0), "zh", n_zh)
        blocks = jnp.sum(heard[:, :n_direct], axis=0).reshape(n_zh, half, TILE) + heard[:, n_direct : n_direct + half]
        sums = jnp.sum(heard[:, n_direct + half :], axis=0)
        mine = lax.dynamic_index_in_dim(blocks, lax.axis_index("zh"), 0, False)
        from_chips = gather_chips(mine)
        from_col = lax.all_gather(jnp.concatenate([blocks.reshape(n_direct, TILE), sums], axis=0), "y", axis=0)
        sums = from_col[:, n_direct:].reshape(n_y * sums_rows, TILE)
        return lax.all_gather(jnp.concatenate([from_chips, sums], axis=0), "core", axis=0), from_col

    def apply_locally(keep, give, y_blocks):
        mirrored, along_y = reduce_row_and_y(keep, give, y_blocks)
        sums = jnp.broadcast_to(mirrored[None, half:], (n_zh, sums_rows, TILE))
        blocks = along_y.reshape(n_zh, half, TILE)
        along_z = jnp.sum(exchange(jnp.concatenate([blocks, sums], axis=1), "zh"), axis=0)
        sums = spread(along_z[half:], "y", n_y).reshape(n_y * sums_rows, TILE)
        return along_z[:half] + mirrored[:half], lax.all_gather(sums, "core", axis=0)

    start = jnp.concatenate([initial_block[:half], initial_block[half:]], axis=1)
    along_z = spread(start, "zh", n_zh)
    from_chips = gather_chips(start)
    from_col = lax.all_gather(along_z.reshape(n_direct, TILE), "y", axis=0)
    from_row = lax.all_gather(from_chips, "core", axis=0)
    trial, *messages = pl.pallas_call(
        functools.partial(first_kernel, n_row, n_col),
        out_shape=(state,) + sends,
        in_specs=[smem] * 3 + [vmem] * 3,
        out_specs=(hbm,) + (vmem,) * 3,
        scratch_shapes=[gathered] + partial_sums + [pltpu.SemaphoreType.DMA],
        compiler_params=params,
    )(where, rows, cols, tiles, from_row, from_col)
    carried = [trial]
    for step in range(ITERS):
        from_row, from_col = apply_and_gather(*messages)
        stored = STORED[step]
        kept = stored or 2
        carried = [pltpu.with_memory_space_constraint(array, pltpu.HBM) for array in carried]
        results = pl.pallas_call(
            functools.partial(middle_kernel, step, n_row, n_col),
            out_shape=((state,) * stored or (own_tile,) * 2) + sends,
            in_specs=[smem] * 3 + [vmem] * 3 + [hbm] * len(carried),
            out_specs=((hbm,) * stored or (vmem,) * 2) + (vmem,) * 3,
            scratch_shapes=[pltpu.VMEM((4, n_tiles, VEC, TILE), f32), gathered]
            + partial_sums
            + [pltpu.SemaphoreType.DMA((4, PIECES)), pltpu.SemaphoreType.DMA((4, PIECES))],
            input_output_aliases={6 + k: k for k in range(min(len(carried), stored))},
            compiler_params=params,
        )(where, rows, cols, tiles, from_row, from_col, *carried)
        carried, messages = results[:kept], results[kept:]
    local, sums = apply_locally(*messages)
    small = jax.ShapeDtypeStruct((VEC, VEC), f32)
    return pl.pallas_call(
        functools.partial(last_kernel, n_y),
        out_shape=(small,) * 3,
        in_specs=[smem] + [vmem] * 4,
        out_specs=(vmem,) * 3,
        compiler_params=params,
    )(where, sums, local, *carried)


def solution(mesh, split=SPLIT):
    fine = Mesh(mesh.devices.reshape(split), AXES)
    in_specs = (
        P(None, AXES),
        P(ROW, COL, None, None, None),
        P(ROW, COL, None),
        P(ROW, COL, None),
    )
    out_specs = (P(None, AXES), P(), P(None, AXES))
    return jax.shard_map(
        functools.partial(per_device, split),
        mesh=fine,
        in_specs=in_specs,
        out_specs=out_specs,
        check_vma=False,
    )
```

profile of v0, /device:TPU:1, one launch (start us, length us, event | category | flops | bytes accessed | tf_op | source)
XLA Modules:
  0.0 483.8 jit_solution(561337516594637452)
XLA Ops:
  1.5 27.9 %all_to_all.110 = f32[4,32,128]{2,1,0:T(8,128)S(1)} all-to-all(f32[4,32,128]{2,1,0:T(8,128)S(1)} %broadcast_in_dim.43), channel_id=1, replica_groups=mesh['x'=4,'zl'=4,'core'=2,'zh'=4,'y'=4] {'zh'}, dimensions={0} | all-to-all | bytes 131072 | tf_op jit(solution)/shard_map/all_to_all | solution.py:344
  30.1 5.5 %all-to-all-start = ((f32[16,32,128]{2,1,0:T(8,128)}), f32[16,32,128]{2,1,0:T(8,128)S(1)}, u32[]{:S(2)}, u32[]{:S(2)}) async-start(f32[16,32,128]{2,1,0:T(8,128)} %broadcast_in_dim.42), calls=%async_computation | async-start | bytes 524288 | tf_op jit(solution)/shard_map/all_to_all | solution.py:344
  35.7 10.2 %all_gather.58.recv_col_ref = f32[4,128,128]{2,1,0:T(8,128)S(1)} all-gather(f32[1,128,128]{2,1,0:T(8,128)S(1)} %bitcast.83), channel_id=1, replica_groups=mesh['x'=4,'zl'=4,'core'=2,'zh'=4,'y'=4] {'y'}, dimensions={0}, use_global_device_ids=true | all-gather | bytes 327680 | tf_op jit(solution)/shard_map/all_gather | solution.py:382
  45.9 7.1 %all_gather.57.recv_row_ref = f32[2,512,128]{2,1,0:T(8,128)S(1)} all-gather(f32[1,512,128]{2,1,0:T(8,128)S(1)} %bitcast.69), channel_id=1, replica_groups=mesh['x'=4,'zl'=4,'core'=2,'zh'=4,'y'=4] {'core'}, dimensions={0}, use_global_device_ids=true | all-gather | bytes 786432 | tf_op jit(solution)/shard_map/all_gather | solution.py:383
  53.7 3.7 shard_map.67
  59.7 3.5 all-to-all-start.2
  63.2 6.8 %all-to-all-done.2 = f32[4,144,128]{2,1,0:T(8,128)S(1)} async-done(((f32[4,144,128]{2,1,0:T(8,128)}), f32[4,144,128]{2,1,0:T(8,128)S(1)}, u32[]{:S(2)}, u32[]{:S(2)}) %all-to-all-start.2) | async-done | bytes 294944 | tf_op jit(solution)/shard_map/all_to_all | solution.py:344
  70.9 6.5 %all-to-all-start.3 = ((f32[16,48,128]{2,1,0:T(8,128)}), f32[16,48,128]{2,1,0:T(8,128)S(1)}, u32[]{:S(2)}, u32[]{:S(2)}) async-start(f32[16,48,128]{2,1,0:T(8,128)} %pad_maximum_fusion), calls=%async_computation.3 | async-start | bytes 786432 | tf_op jit(solution)/shard_map/all_to_all | solution.py:344
  77.4 12.4 %all-to-all-done.3 = f32[16,48,128]{2,1,0:T(8,128)S(1)} async-done(((f32[16,48,128]{2,1,0:T(8,128)}), f32[16,48,128]{2,1,0:T(8,128)S(1)}, u32[]{:S(2)}, u32[]{:S(2)}) %all-to-all-start.3) | async-done | bytes 393248 | tf_op jit(solution)/shard_map/all_to_all | solution.py:344
  94.1 19.2 %all-to-all-done.4 = f32[4,176,128]{2,1,0:T(8,128)S(1)} async-done(((f32[4,176,128]{2,1,0:T(8,128)}), f32[4,176,128]{2,1,0:T(8,128)S(1)}, u32[]{:S(2)}, u32[]{:S(2)}) %all-to-all-start.4) | async-done | bytes 360480 | tf_op jit(solution)/shard_map/all_to_all | solution.py:344
  114.1 4.2 all-to-all-start.5
  118.3 9.7 %all-gather = f32[576,128]{1,0:T(8,128)S(1)} all-gather(f32[144,128]{1,0:T(8,128)S(1)} %pad_maximum_fusion.14), channel_id=2, replica_groups=mesh['x'=4,'zl'=4,'core'=2,'zh'=4,'y'=4] {'y'}, dimensions={0}, use_global_device_ids=true | all-gather | bytes 368640 | tf_op jit(solution)/shard_map/all_gather | solution.py:367
  128.1 9.7 %all-gather.1 = f32[1152,128]{1,0:T(8,128)S(1)} all-gather(f32[576,128]{1,0:T(8,128)S(1)} %pad_maximum_fusion.5), channel_id=3, replica_groups=mesh['x'=4,'zl'=4,'core'=2,'zh'=4,'y'=4] {'core'}, dimensions={0}, use_global_device_ids=true | all-gather | bytes 884736 | tf_op jit(solution)/shard_map/all_gather | solution.py:369
  137.8 8.7 %shard_map.68 = (f32[24,64,128]{2,1,0:T(8,128)}, f32[24,64,128]{2,1,0:T(8,128)}, f32[24,64,128]{2,1,0:T(8,128)}, f32[16,32,128]{2,1,0:T(8,128)S(1)}, f32[16,32,128]{2,1,0:T(8,128)S(1)}, /*index=5*/f32[4,144,128]{2,1,0:T(8,128)}) custom-call(s32[3]{0:T(128)S(1)} %pad_add_fusion.where_ref.refs_0_, s32[4]{0:T(128)S(1)} %bitcast.60, ...), custom_call_target="tpu_custom_call", output_to_operand_aliasing={{0}: (6, {})} | custom-call | tf_op jit(solution)/shard_map/pallas_call | solution.py:398
  148.8 3.5 all-to-all-start.6
  152.3 6.9 %all-to-all-done.6 = f32[4,144,128]{2,1,0:T(8,128)S(1)} async-done(((f32[4,144,128]{2,1,0:T(8,128)}), f32[4,144,128]{2,1,0:T(8,128)S(1)}, u32[]{:S(2)}, u32[]{:S(2)}) %all-to-all-start.6) | async-done | bytes 294944 | tf_op jit(solution)/shard_map/all_to_all | solution.py:344
  160.1 7.2 %all-to-all-start.7 = ((f32[16,48,128]{2,1,0:T(8,128)}), f32[16,48,128]{2,1,0:T(8,128)S(1)}, u32[]{:S(2)}, u32[]{:S(2)}) async-start(f32[16,48,128]{2,1,0:T(8,128)} %pad_maximum_fusion.1), calls=%async_computation.7 | async-start | bytes 786432 | tf_op jit(solution)/shard_map/all_to_all | solution.py:344
  167.3 12.9 %all-to-all-done.7 = f32[16,48,128]{2,1,0:T(8,128)S(1)} async-done(((f32[16,48,128]{2,1,0:T(8,128)}), f32[16,48,128]{2,1,0:T(8,128)S(1)}, u32[]{:S(2)}, u32[]{:S(2)}) %all-to-all-start.7) | async-done | bytes 393248 | tf_op jit(solution)/shard_map/all_to_all | solution.py:344
  180.3 23.4 %all_to_all.111 = f32[4,176,128]{2,1,0:T(8,128)S(1)} all-to-all(f32[4,176,128]{2,1,0:T(8,128)S(1)} %broadcast_in_dim.49), channel_id=1, replica_groups=mesh['x'=4,'zl'=4,'core'=2,'zh'=4,'y'=4] {'zh'}, dimensions={0} | all-to-all | bytes 720896 | tf_op jit(solution)/shard_map/all_to_all | solution.py:344
  204.5 4.0 all-to-all-start.9
  208.6 9.7 %all-gather.2 = f32[576,128]{1,0:T(8,128)S(1)} all-gather(f32[144,128]{1,0:T(8,128)S(1)} %pad_maximum_fusion.15), channel_id=4, replica_groups=mesh['x'=4,'zl'=4,'core'=2,'zh'=4,'y'=4] {'y'}, dimensions={0}, use_global_device_ids=true | all-gather | bytes 368640 | tf_op jit(solution)/shard_map/all_gather | solution.py:367
  218.3 9.6 %all-gather.3 = f32[1152,128]{1,0:T(8,128)S(1)} all-gather(f32[576,128]{1,0:T(8,128)S(1)} %pad_maximum_fusion.6), channel_id=5, replica_groups=mesh['x'=4,'zl'=4,'core'=2,'zh'=4,'y'=4] {'core'}, dimensions={0}, use_global_device_ids=true | all-gather | bytes 884736 | tf_op jit(solution)/shard_map/all_gather | solution.py:369
  227.9 9.5 %shard_map.69 = (f32[24,64,128]{2,1,0:T(8,128)}, f32[24,64,128]{2,1,0:T(8,128)}, f32[24,64,128]{2,1,0:T(8,128)}, f32[24,64,128]{2,1,0:T(8,128)}, f32[16,32,128]{...) custom-call(s32[3]{0:T(128)S(1)} %pad_add_fusion.where_ref.refs_0_, ...), custom_call_target="tpu_custom_call", output_to_operand_aliasing={{0}: (6, {}), {1}: (7, {}), {2}: (8, {})} | custom-call | tf_op jit(solution)/shard_map/pallas_call | solution.py:398
  239.7 3.5 all-to-all-start.10
  243.2 6.9 %all-to-all-done.10 = f32[4,144,128]{2,1,0:T(8,128)S(1)} async-done(((f32[4,144,128]{2,1,0:T(8,128)}), f32[4,144,128]{2,1,0:T(8,128)S(1)}, u32[]{:S(2)}, u32[]{:S(2)}) %all-to-all-start.10) | async-done | bytes 294944 | tf_op jit(solution)/shard_map/all_to_all | solution.py:344
  251.0 7.2 %all-to-all-start.11 = ((f32[16,48,128]{2,1,0:T(8,128)}), f32[16,48,128]{2,1,0:T(8,128)S(1)}, u32[]{:S(2)}, u32[]{:S(2)}) async-start(f32[16,48,128]{2,1,0:T(8,128)} %pad_maximum_fusion.2), calls=%async_computation.11 | async-start | bytes 786432 | tf_op jit(solution)/shard_map/all_to_all | solution.py:344
  258.2 12.9 %all-to-all-done.11 = f32[16,48,128]{2,1,0:T(8,128)S(1)} async-done(((f32[16,48,128]{2,1,0:T(8,128)}), f32[16,48,128]{2,1,0:T(8,128)S(1)}, u32[]{:S(2)}, u32[]{:S(2)}) %all-to-all-start.11) | async-done | bytes 393248 | tf_op jit(solution)/shard_map/all_to_all | solution.py:344
  271.2 22.9 %all_to_all.112 = f32[4,176,128]{2,1,0:T(8,128)S(1)} all-to-all(f32[4,176,128]{2,1,0:T(8,128)S(1)} %broadcast_in_dim.53), channel_id=1, replica_groups=mesh['x'=4,'zl'=4,'core'=2,'zh'=4,'y'=4] {'zh'}, dimensions={0} | all-to-all | bytes 720896 | tf_op jit(solution)/shard_map/all_to_all | solution.py:344
  294.9 4.0 all-to-all-start.13
  298.9 9.7 %all-gather.4 = f32[576,128]{1,0:T(8,128)S(1)} all-gather(f32[144,128]{1,0:T(8,128)S(1)} %pad_maximum_fusion.16), channel_id=6, replica_groups=mesh['x'=4,'zl'=4,'core'=2,'zh'=4,'y'=4] {'y'}, dimensions={0}, use_global_device_ids=true | all-gather | bytes 368640 | tf_op jit(solution)/shard_map/all_gather | solution.py:367
  308.7 9.4 %all-gather.5 = f32[1152,128]{1,0:T(8,128)S(1)} all-gather(f32[576,128]{1,0:T(8,128)S(1)} %pad_maximum_fusion.7), channel_id=7, replica_groups=mesh['x'=4,'zl'=4,'core'=2,'zh'=4,'y'=4] {'core'}, dimensions={0}, use_global_device_ids=true | all-gather | bytes 884736 | tf_op jit(solution)/shard_map/all_gather | solution.py:369
  318.1 9.2 %shard_map.70 = (f32[24,64,128]{2,1,0:T(8,128)}, f32[24,64,128]{2,1,0:T(8,128)}, f32[24,64,128]{2,1,0:T(8,128)}, f32[24,64,128]{2,1,0:T(8,128)}, f32[16,32,128]{...) custom-call(s32[3]{0:T(128)S(1)} %pad_add_fusion.where_ref.refs_0_, ...), custom_call_target="tpu_custom_call", output_to_operand_aliasing={{0}: (6, {}), {1}: (7, {}), {2}: (8, {}), {3}: (9, {})} | custom-call | tf_op jit(solution)/shard_map/pallas_call | solution.py:398
  329.6 3.5 all-to-all-start.14
  333.1 6.9 %all-to-all-done.14 = f32[4,144,128]{2,1,0:T(8,128)S(1)} async-done(((f32[4,144,128]{2,1,0:T(8,128)}), f32[4,144,128]{2,1,0:T(8,128)S(1)}, u32[]{:S(2)}, u32[]{:S(2)}) %all-to-all-start.14) | async-done | bytes 294944 | tf_op jit(solution)/shard_map/all_to_all | solution.py:344
  340.9 7.2 %all-to-all-start.15 = ((f32[16,48,128]{2,1,0:T(8,128)}), f32[16,48,128]{2,1,0:T(8,128)S(1)}, u32[]{:S(2)}, u32[]{:S(2)}) async-start(f32[16,48,128]{2,1,0:T(8,128)} %pad_maximum_fusion.3), calls=%async_computation.15 | async-start | bytes 786432 | tf_op jit(solution)/shard_map/all_to_all | solution.py:344
  348.1 12.9 %all-to-all-done.15 = f32[16,48,128]{2,1,0:T(8,128)S(1)} async-done(((f32[16,48,128]{2,1,0:T(8,128)}), f32[16,48,128]{2,1,0:T(8,128)S(1)}, u32[]{:S(2)}, u32[]{:S(2)}) %all-to-all-start.15) | async-done | bytes 393248 | tf_op jit(solution)/shard_map/all_to_all | solution.py:344
  361.1 22.9 %all_to_all.113 = f32[4,176,128]{2,1,0:T(8,128)S(1)} all-to-all(f32[4,176,128]{2,1,0:T(8,128)S(1)} %broadcast_in_dim.57), channel_id=1, replica_groups=mesh['x'=4,'zl'=4,'core'=2,'zh'=4,'y'=4] {'zh'}, dimensions={0} | all-to-all | bytes 720896 | tf_op jit(solution)/shard_map/all_to_all | solution.py:344
  384.8 4.0 all-to-all-start.17
  388.8 9.7 %all-gather.6 = f32[576,128]{1,0:T(8,128)S(1)} all-gather(f32[144,128]{1,0:T(8,128)S(1)} %pad_maximum_fusion.17), channel_id=8, replica_groups=mesh['x'=4,'zl'=4,'core'=2,'zh'=4,'y'=4] {'y'}, dimensions={0}, use_global_device_ids=true | all-gather | bytes 368640 | tf_op jit(solution)/shard_map/all_gather | solution.py:367
  398.6 9.4 %all-gather.7 = f32[1152,128]{1,0:T(8,128)S(1)} all-gather(f32[576,128]{1,0:T(8,128)S(1)} %pad_maximum_fusion.8), channel_id=9, replica_groups=mesh['x'=4,'zl'=4,'core'=2,'zh'=4,'y'=4] {'core'}, dimensions={0}, use_global_device_ids=true | all-gather | bytes 884736 | tf_op jit(solution)/shard_map/all_gather | solution.py:369
  408.0 8.9 %shard_map.71 = (f32[64,128]{1,0:T(8,128)S(1)}, f32[64,128]{1,0:T(8,128)S(1)}, f32[16,32,128]{2,1,0:T(8,128)S(1)}, f32[16,32,128]{2,1,0:T(8,128)S(1)}, f32[4,144,128]{2,1,0:T(8,128)}) custom-call(s32[3]{0:T(128)S(1)} %pad_add_fusion.where_ref.refs_0_, s32[4]{0:T(128)S(1)} %bitcast.63, s32[4]{0:T(128)S(1)} %bitcast.68, f32[4,128,128]{2,1,0:T(8,128)S(1)} %bitcast.46, ...), custom_call_target="tpu_custom_call" | custom-call | tf_op jit(solution)/shard_map/pallas_call | solution.py:398
  422.7 6.9 %all-to-all-done.18 = f32[4,144,128]{2,1,0:T(8,128)S(1)} async-done(((f32[4,144,128]{2,1,0:T(8,128)}), f32[4,144,128]{2,1,0:T(8,128)S(1)}, u32[]{:S(2)}, u32[]{:S(2)}) %all-to-all-start.18) | async-done | bytes 294944 | tf_op jit(solution)/shard_map/all_to_all | solution.py:344
  430.5 7.2 %all-to-all-start.19 = ((f32[16,48,128]{2,1,0:T(8,128)}), f32[16,48,128]{2,1,0:T(8,128)S(1)}, u32[]{:S(2)}, u32[]{:S(2)}) async-start(f32[16,48,128]{2,1,0:T(8,128)} %pad_maximum_fusion.4), calls=%async_computation.19 | async-start | bytes 786432 | tf_op jit(solution)/shard_map/all_to_all | solution.py:344
  437.7 12.9 %all-to-all-done.19 = f32[16,48,128]{2,1,0:T(8,128)S(1)} async-done(((f32[16,48,128]{2,1,0:T(8,128)}), f32[16,48,128]{2,1,0:T(8,128)S(1)}, u32[]{:S(2)}, u32[]{:S(2)}) %all-to-all-start.19) | async-done | bytes 393248 | tf_op jit(solution)/shard_map/all_to_all | solution.py:344
  451.5 14.5 %all_to_all.114 = f32[4,48,128]{2,1,0:T(8,128)S(1)} all-to-all(f32[4,48,128]{2,1,0:T(8,128)S(1)} %pad_maximum_fusion.9), channel_id=1, replica_groups=mesh['x'=4,'zl'=4,'core'=2,'zh'=4,'y'=4] {'zh'}, dimensions={0} | all-to-all | bytes 196608 | tf_op jit(solution)/shard_map/all_to_all | solution.py:344
  469.9 4.3 all-to-all-done.21
  474.2 5.7 %all_gather.75.recv_ref = f32[2,64,128]{2,1,0:T(8,128)S(1)} all-gather(f32[1,64,128]{2,1,0:T(8,128)S(1)} %bitcast.84), channel_id=1, replica_groups=mesh['x'=4,'zl'=4,'core'=2,'zh'=4,'y'=4] {'core'}, dimensions={0}, use_global_device_ids=true | all-gather | bytes 98304 | tf_op jit(solution)/shard_map/all_gather | solution.py:377
  479.9 3.9 shard_map.72
  (126 shorter events, 33.9 us)
Async XLA Ops:
  30.1 15.8 %all-to-all-start = ((f32[16,32,128]{2,1,0:T(8,128)}), f32[16,32,128]{2,1,0:T(8,128)S(1)}, u32[]{:S(2)}, u32[]{:S(2)}) async-start(f32[16,32,128]{2,1,0:T(8,128)} %broadcast_in_dim.42), calls=%async_computation | async-start | bytes 524288 | tf_op jit(solution)/shard_map/all_to_all | solution.py:344
  45.9 7.1 %copy-start = (f32[1,1,4,128,128]{4,3,2,1,0:T(8,128)S(1)}, f32[1,1,4,128,128]{4,3,2,1,0:T(8,128)}, u32[]{:S(2)}) copy-start(f32[1,1,4,128,128]{4,3,2,1,0:T(8,128)} %param.5) | copy-start | bytes 786436
  53.0 0.7 copy-start.1
  53.0 0.7 copy-start.2
  57.4 5.8 %collective-permute-start = (f32[16,32,128]{2,1,0:T(8,128)S(1)}, f32[16,32,128]{2,1,0:T(8,128)S(1)}, u32[]{:S(2)}, u32[]{:S(2)}) collective-permute-start(f32[16,32,128]{2,1,0:T(8,128)S(1)} %get-tuple-element.44), channel_id=1, source_target_pairs={{0,16},{16,0},{1,17},{17,1},{2,18},{18,2},{3,19},{19,3},{4,20},{20... | collective-permute-start | bytes 786440 | tf_op jit(solution)/shard_map/ppermute | solution.py:350
  59.7 10.4 %all-to-all-start.2 = ((f32[4,144,128]{2,1,0:T(8,128)}), f32[4,144,128]{2,1,0:T(8,128)S(1)}, u32[]{:S(2)}, u32[]{:S(2)}) async-start(f32[4,144,128]{2,1,0:T(8,128)} %get-tuple-element.42), calls=%async_computation.2 | async-start | bytes 589824 | tf_op jit(solution)/shard_map/all_to_all | solution.py:344
  70.1 7.3 %copy-start.3 = (f32[144,128]{1,0:T(8,128)}, f32[144,128]{1,0:T(8,128)S(1)}, u32[]{:S(2)}) copy-start(f32[144,128]{1,0:T(8,128)S(1)} %reduce_sum.171) | copy-start | bytes 221188
  70.9 18.9 %all-to-all-start.3 = ((f32[16,48,128]{2,1,0:T(8,128)}), f32[16,48,128]{2,1,0:T(8,128)S(1)}, u32[]{:S(2)}, u32[]{:S(2)}) async-start(f32[16,48,128]{2,1,0:T(8,128)} %pad_maximum_fusion), calls=%async_computation.3 | async-start | bytes 786432 | tf_op jit(solution)/shard_map/all_to_all | solution.py:344
  77.4 12.4 %slice-start = ((f32[144,128]{1,0:T(8,128)}), f32[128,128]{1,0:T(8,128)S(1)}, s32[]{:S(2)}) async-start(f32[144,128]{1,0:T(8,128)} %copy-done.3), calls=%async_computation.22 | async-start | bytes 131072 | tf_op jit(solution)/shard_map/slice | solution.py:355
  90.6 22.7 %all-to-all-start.4 = ((f32[4,176,128]{2,1,0:T(8,128)}), f32[4,176,128]{2,1,0:T(8,128)S(1)}, u32[]{:S(2)}, u32[]{:S(2)}) async-start(f32[4,176,128]{2,1,0:T(8,128)} %broadcast_in_dim.45), calls=%async_computation.4 | async-start | bytes 720896 | tf_op jit(solution)/shard_map/all_to_all | solution.py:344
  114.1 14.0 %all-to-all-start.5 = ((f32[16,32,128]{2,1,0:T(8,128)}), f32[16,32,128]{2,1,0:T(8,128)S(1)}, u32[]{:S(2)}, u32[]{:S(2)}) async-start(f32[16,32,128]{2,1,0:T(8,128)} %broadcast_in_dim.47), calls=%async_computation.5 | async-start | bytes 524288 | tf_op jit(solution)/shard_map/all_to_all | solution.py:344
  146.5 5.8 %collective-permute-start.1 = (f32[16,32,128]{2,1,0:T(8,128)S(1)}, f32[16,32,128]{2,1,0:T(8,128)S(1)}, u32[]{:S(2)}, u32[]{:S(2)}) collective-permute-start(f32[16,32,128]{2,1,0:T(8,128)S(1)} %get-tuple-element.50), channel_id=1, source_target_pairs={{0,16},{16,0},{1,17},{17,1},{2,18},{18,2},{3,19},{19,3},{4,20},{20... | collective-permute-start | bytes 786440 | tf_op jit(solution)/shard_map/ppermute | solution.py:350
  148.8 10.5 %all-to-all-start.6 = ((f32[4,144,128]{2,1,0:T(8,128)}), f32[4,144,128]{2,1,0:T(8,128)S(1)}, u32[]{:S(2)}, u32[]{:S(2)}) async-start(f32[4,144,128]{2,1,0:T(8,128)} %get-tuple-element.48), calls=%async_computation.6 | async-start | bytes 589824 | tf_op jit(solution)/shard_map/all_to_all | solution.py:344
  159.3 8.0 %copy-start.4 = (f32[144,128]{1,0:T(8,128)}, f32[144,128]{1,0:T(8,128)S(1)}, u32[]{:S(2)}) copy-start(f32[144,128]{1,0:T(8,128)S(1)} %reduce_sum.175) | copy-start | bytes 221188
  160.1 20.1 %all-to-all-start.7 = ((f32[16,48,128]{2,1,0:T(8,128)}), f32[16,48,128]{2,1,0:T(8,128)S(1)}, u32[]{:S(2)}, u32[]{:S(2)}) async-start(f32[16,48,128]{2,1,0:T(8,128)} %pad_maximum_fusion.1), calls=%async_computation.7 | async-start | bytes 786432 | tf_op jit(solution)/shard_map/all_to_all | solution.py:344
  167.3 12.9 %slice-start.1 = ((f32[144,128]{1,0:T(8,128)}), f32[128,128]{1,0:T(8,128)S(1)}, s32[]{:S(2)}) async-start(f32[144,128]{1,0:T(8,128)} %copy-done.4), calls=%async_computation.23 | async-start | bytes 131072 | tf_op jit(solution)/shard_map/slice | solution.py:355
  204.5 13.8 %all-to-all-start.9 = ((f32[16,32,128]{2,1,0:T(8,128)}), f32[16,32,128]{2,1,0:T(8,128)S(1)}, u32[]{:S(2)}, u32[]{:S(2)}) async-start(f32[16,32,128]{2,1,0:T(8,128)} %broadcast_in_dim.51), calls=%async_computation.9 | async-start | bytes 524288 | tf_op jit(solution)/shard_map/all_to_all | solution.py:344
  237.4 5.8 %collective-permute-start.2 = (f32[16,32,128]{2,1,0:T(8,128)S(1)}, f32[16,32,128]{2,1,0:T(8,128)S(1)}, u32[]{:S(2)}, u32[]{:S(2)}) collective-permute-start(f32[16,32,128]{2,1,0:T(8,128)S(1)} %get-tuple-element.58), channel_id=1, source_target_pairs={{0,16},{16,0},{1,17},{17,1},{2,18},{18,2},{3,19},{19,3},{4,20},{20... | collective-permute-start | bytes 786440 | tf_op jit(solution)/shard_map/ppermute | solution.py:350
  239.7 10.5 %all-to-all-start.10 = ((f32[4,144,128]{2,1,0:T(8,128)}), f32[4,144,128]{2,1,0:T(8,128)S(1)}, u32[]{:S(2)}, u32[]{:S(2)}) async-start(f32[4,144,128]{2,1,0:T(8,128)} %get-tuple-element.56), calls=%async_computation.10 | async-start | bytes 589824 | tf_op jit(solution)/shard_map/all_to_all | solution.py:344
  250.2 8.0 %copy-start.5 = (f32[144,128]{1,0:T(8,128)}, f32[144,128]{1,0:T(8,128)S(1)}, u32[]{:S(2)}) copy-start(f32[144,128]{1,0:T(8,128)S(1)} %reduce_sum.179) | copy-start | bytes 221188
  251.0 20.1 %all-to-all-start.11 = ((f32[16,48,128]{2,1,0:T(8,128)}), f32[16,48,128]{2,1,0:T(8,128)S(1)}, u32[]{:S(2)}, u32[]{:S(2)}) async-start(f32[16,48,128]{2,1,0:T(8,128)} %pad_maximum_fusion.2), calls=%async_computation.11 | async-start | bytes 786432 | tf_op jit(solution)/shard_map/all_to_all | solution.py:344
  258.2 12.9 %slice-start.2 = ((f32[144,128]{1,0:T(8,128)}), f32[128,128]{1,0:T(8,128)S(1)}, s32[]{:S(2)}) async-start(f32[144,128]{1,0:T(8,128)} %copy-done.5), calls=%async_computation.24 | async-start | bytes 131072 | tf_op jit(solution)/shard_map/slice | solution.py:355
  294.9 13.8 %all-to-all-start.13 = ((f32[16,32,128]{2,1,0:T(8,128)}), f32[16,32,128]{2,1,0:T(8,128)S(1)}, u32[]{:S(2)}, u32[]{:S(2)}) async-start(f32[16,32,128]{2,1,0:T(8,128)} %broadcast_in_dim.55), calls=%async_computation.13 | async-start | bytes 524288 | tf_op jit(solution)/shard_map/all_to_all | solution.py:344
  327.3 5.8 %collective-permute-start.3 = (f32[16,32,128]{2,1,0:T(8,128)S(1)}, f32[16,32,128]{2,1,0:T(8,128)S(1)}, u32[]{:S(2)}, u32[]{:S(2)}) collective-permute-start(f32[16,32,128]{2,1,0:T(8,128)S(1)} %get-tuple-element.67), channel_id=1, source_target_pairs={{0,16},{16,0},{1,17},{17,1},{2,18},{18,2},{3,19},{19,3},{4,20},{20... | collective-permute-start | bytes 786440 | tf_op jit(solution)/shard_map/ppermute | solution.py:350
  329.6 10.5 %all-to-all-start.14 = ((f32[4,144,128]{2,1,0:T(8,128)}), f32[4,144,128]{2,1,0:T(8,128)S(1)}, u32[]{:S(2)}, u32[]{:S(2)}) async-start(f32[4,144,128]{2,1,0:T(8,128)} %get-tuple-element.65), calls=%async_computation.14 | async-start | bytes 589824 | tf_op jit(solution)/shard_map/all_to_all | solution.py:344
  340.1 8.1 %copy-start.6 = (f32[144,128]{1,0:T(8,128)}, f32[144,128]{1,0:T(8,128)S(1)}, u32[]{:S(2)}) copy-start(f32[144,128]{1,0:T(8,128)S(1)} %reduce_sum.183) | copy-start | bytes 221188
  340.9 20.1 %all-to-all-start.15 = ((f32[16,48,128]{2,1,0:T(8,128)}), f32[16,48,128]{2,1,0:T(8,128)S(1)}, u32[]{:S(2)}, u32[]{:S(2)}) async-start(f32[16,48,128]{2,1,0:T(8,128)} %pad_maximum_fusion.3), calls=%async_computation.15 | async-start | bytes 786432 | tf_op jit(solution)/shard_map/all_to_all | solution.py:344
  348.1 12.9 %slice-start.3 = ((f32[144,128]{1,0:T(8,128)}), f32[128,128]{1,0:T(8,128)S(1)}, s32[]{:S(2)}) async-start(f32[144,128]{1,0:T(8,128)} %copy-done.6), calls=%async_computation.25 | async-start | bytes 131072 | tf_op jit(solution)/shard_map/slice | solution.py:355
  384.8 13.8 %all-to-all-start.17 = ((f32[16,32,128]{2,1,0:T(8,128)}), f32[16,32,128]{2,1,0:T(8,128)S(1)}, u32[]{:S(2)}, u32[]{:S(2)}) async-start(f32[16,32,128]{2,1,0:T(8,128)} %broadcast_in_dim.59), calls=%async_computation.17 | async-start | bytes 524288 | tf_op jit(solution)/shard_map/all_to_all | solution.py:344
  416.9 5.8 %collective-permute-start.4 = (f32[16,32,128]{2,1,0:T(8,128)S(1)}, f32[16,32,128]{2,1,0:T(8,128)S(1)}, u32[]{:S(2)}, u32[]{:S(2)}) collective-permute-start(f32[16,32,128]{2,1,0:T(8,128)S(1)} %get-tuple-element.76), channel_id=1, source_target_pairs={{0,16},{16,0},{1,17},{17,1},{2,18},{18,2},{3,19},{19,3},{4,20},{20... | collective-permute-start | bytes 786440 | tf_op jit(solution)/shard_map/ppermute | solution.py:350
  419.2 10.4 %all-to-all-start.18 = ((f32[4,144,128]{2,1,0:T(8,128)}), f32[4,144,128]{2,1,0:T(8,128)S(1)}, u32[]{:S(2)}, u32[]{:S(2)}) async-start(f32[4,144,128]{2,1,0:T(8,128)} %get-tuple-element.74), calls=%async_computation.18 | async-start | bytes 589824 | tf_op jit(solution)/shard_map/all_to_all | solution.py:344
  429.7 8.1 %copy-start.7 = (f32[144,128]{1,0:T(8,128)}, f32[144,128]{1,0:T(8,128)S(1)}, u32[]{:S(2)}) copy-start(f32[144,128]{1,0:T(8,128)S(1)} %reduce_sum.187) | copy-start | bytes 221188
  430.5 20.1 %all-to-all-start.19 = ((f32[16,48,128]{2,1,0:T(8,128)}), f32[16,48,128]{2,1,0:T(8,128)S(1)}, u32[]{:S(2)}, u32[]{:S(2)}) async-start(f32[16,48,128]{2,1,0:T(8,128)} %pad_maximum_fusion.4), calls=%async_computation.19 | async-start | bytes 786432 | tf_op jit(solution)/shard_map/all_to_all | solution.py:344
  450.6 0.8 slice-start.4
  466.7 7.5 %all-to-all-start.21 = ((f32[4,16,128]{2,1,0:T(8,128)}), f32[4,16,128]{2,1,0:T(8,128)S(1)}, u32[]{:S(2)}, u32[]{:S(2)}) async-start(f32[4,16,128]{2,1,0:T(8,128)} %broadcast_in_dim.62), calls=%async_computation.21 | async-start | bytes 65536 | tf_op jit(solution)/shard_map/all_to_all | solution.py:344
where the time goes:
time: 486 us; the launch traced here: 484 us
  blocking collectives  212 us (44%)
  waiting for transfers between devices  122 us (25%)
  starting transfers between devices  92.5 us (19%)
  Pallas kernels  44 us (9%)
  local copies, waits for them, and re-layouts  7.47 us (2%)
    all_to_all x17, waiting for transfers between devices, exchange(): return lax.all_to_all(blocks, axes, 0, 0, tiled=True)  122 us
    all_to_all x5, blocking collectives, exchange(): return lax.all_to_all(blocks, axes, 0, 0, tiled=True)  112 us
    all_to_all x17, starting transfers between devices, exchange(): return lax.all_to_all(blocks, axes, 0, 0, tiled=True)  81.1 us
    all_gather x4, blocking collectives, apply_and_gather(): lax.all_gather(jnp.concatenate([blocks.reshape(n_direct, TILE), sums], ax...  38.9 us
    all_gather x4, blocking collectives, apply_and_gather(): lax.all_gather(jnp.concatenate([from_chips, sums], axis=0), 'core', axis=0)  38 us
    pallas_call x4, Pallas kernels, per_device(): pl.pallas_call(functools.partial(middle_kernel, step, n_row, n_col), out_...  36.4 us
    ppermute x5, starting transfers between devices, reduce_row_and_y(): both_cores = keep + lax.ppermute(give, 'core', [(0, 1), (1, 0)])  11.4 us
    all_gather x1, blocking collectives, per_device(): from_col = lax.all_gather(along_z.reshape(n_direct, TILE), 'y', axis=0)  10.2 us
  transfers between devices with their start and end apart: 22, of which 12 were waited for; matrix products, arithmetic and copies ran while one was open for 0% of the time, Pallas kernels for 0%

commit v1 on v0

--- a/solution.py
+++ b/solution.py
@@ -348,11 +348,11 @@
 
     def reduce_row_and_y(keep, give, y_blocks):
         both_cores = keep + lax.ppermute(give, "core", [(0, 1), (1, 0)])
-        from_y, both_cores = lax.optimization_barrier((exchange(y_blocks, "y"), both_cores))
-        along_y = jnp.sum(from_y, axis=0)
+        along_y = jnp.sum(exchange(y_blocks, "y"), axis=0)
         sums = jnp.broadcast_to(along_y[None, n_direct:], (n_row // 2, sums_rows, TILE))
-        mirrored = jnp.sum(exchange(jnp.concatenate([both_cores, sums], axis=1), CHIPS), axis=0)
-        return mirrored, along_y[:n_direct]
+        from_chips = exchange(jnp.concatenate([both_cores, sums], axis=1), CHIPS)
+        from_chips, along_y = lax.optimization_barrier((from_chips, along_y))
+        return jnp.sum(from_chips, axis=0), along_y[:n_direct]
 
     def gather_chips(block):
         return spread(block, CHIPS, n_row // 2).reshape(n_row // 2 * half, TILE)

time: 486 us -> 475 us (0.977)
  blocking collectives: 212 us -> 353 us
  waiting for transfers between devices: 122 us -> 23.3 us
  starting transfers between devices: 92.5 us -> 43.4 us
    all_to_all x5 -> x15, blocking collectives: 112 us -> 253 us  [exchange(): return lax.all_to_all(blocks, axes, 0, 0, tiled=True)]
    all_to_all x17 -> x7, waiting for transfers between devices: 122 us -> 23.2 us  [exchange(): return lax.all_to_all(blocks, axes, 0, 0, tiled=True)]
    all_to_all x17 -> x7, starting transfers between devices: 81.1 us -> 31.9 us  [exchange(): return lax.all_to_all(blocks, axes, 0, 0, tiled=True)]
  transfers between devices with their start and end apart: 22 -> 12, of which waited for: 12 -> 2; matrix products, arithmetic and copies ran while one was open for 0% -> 0% of each run, Pallas kernels for 0% -> 0%
where the time goes in v1:
time: 475 us; the launch traced here: 473 us
  blocking collectives  353 us (74%)
  starting transfers between devices  43.4 us (9%)
  Pallas kernels  40.4 us (9%)
  waiting for transfers between devices  23.3 us (5%)
  local copies, waits for them, and re-layouts  10.7 us (2%)
    all_to_all x15, blocking collectives, exchange(): return lax.all_to_all(blocks, axes, 0, 0, tiled=True)  253 us
    all_gather x4, blocking collectives, apply_and_gather(): lax.all_gather(jnp.concatenate([blocks.reshape(n_direct, TILE), sums], ax...  39.4 us
    all_gather x4, blocking collectives, apply_and_gather(): lax.all_gather(jnp.concatenate([from_chips, sums], axis=0), 'core', axis=0)  36.9 us
    pallas_call x4, Pallas kernels, per_device(): pl.pallas_call(functools.partial(middle_kernel, step, n_row, n_col), out_...  33.6 us
    all_to_all x7, starting transfers between devices, exchange(): return lax.all_to_all(blocks, axes, 0, 0, tiled=True)  31.9 us
    all_to_all x7, waiting for transfers between devices, exchange(): return lax.all_to_all(blocks, axes, 0, 0, tiled=True)  23.2 us
    ppermute x5, starting transfers between devices, reduce_row_and_y(): both_cores = keep + lax.ppermute(give, 'core', [(0, 1), (1, 0)])  11.4 us
    all_gather x1, blocking collectives, per_device(): from_col = lax.all_gather(along_z.reshape(n_direct, TILE), 'y', axis=0)  10.2 us
  transfers between devices with their start and end apart: 12, of which 2 were waited for; matrix products, arithmetic and copies ran while one was open for 0% of the time, Pallas kernels for 0%

profile of v1, /device:TPU:1, one launch (start us, length us, event | category | flops | bytes accessed | tf_op | source)
XLA Modules:
  0.0 472.9 jit_solution(16088420581442741410)
XLA Ops:
  1.5 27.9 %all_to_all.110 = f32[4,32,128]{2,1,0:T(8,128)S(1)} all-to-all(f32[4,32,128]{2,1,0:T(8,128)S(1)} %broadcast_in_dim.43), channel_id=1, replica_groups=mesh['x'=4,'zl'=4,'core'=2,'zh'=4,'y'=4] {'zh'}, dimensions={0} | all-to-all | bytes 131072 | tf_op jit(solution)/shard_map/all_to_all | solution.py:344
  30.1 5.5 %all-to-all-start = ((f32[16,32,128]{2,1,0:T(8,128)}), f32[16,32,128]{2,1,0:T(8,128)S(1)}, u32[]{:S(2)}, u32[]{:S(2)}) async-start(f32[16,32,128]{2,1,0:T(8,128)} %broadcast_in_dim.42), calls=%async_computation | async-start | bytes 524288 | tf_op jit(solution)/shard_map/all_to_all | solution.py:344
  35.7 10.2 %all_gather.58.recv_col_ref = f32[4,128,128]{2,1,0:T(8,128)S(1)} all-gather(f32[1,128,128]{2,1,0:T(8,128)S(1)} %bitcast.83), channel_id=1, replica_groups=mesh['x'=4,'zl'=4,'core'=2,'zh'=4,'y'=4] {'y'}, dimensions={0}, use_global_device_ids=true | all-gather | bytes 327680 | tf_op jit(solution)/shard_map/all_gather | solution.py:382
  45.9 7.1 %all_gather.57.recv_row_ref = f32[2,512,128]{2,1,0:T(8,128)S(1)} all-gather(f32[1,512,128]{2,1,0:T(8,128)S(1)} %bitcast.69), channel_id=1, replica_groups=mesh['x'=4,'zl'=4,'core'=2,'zh'=4,'y'=4] {'core'}, dimensions={0}, use_global_device_ids=true | all-gather | bytes 786432 | tf_op jit(solution)/shard_map/all_gather | solution.py:383
  53.7 2.9 shard_map.67
  56.5 2.3 collective-permute-start
  58.8 9.7 %all_to_all.111 = f32[4,144,128]{2,1,0:T(8,128)S(1)} all-to-all(f32[4,144,128]{2,1,0:T(8,128)S(1)} %get-tuple-element.44), channel_id=1, replica_groups=mesh['x'=4,'zl'=4,'core'=2,'zh'=4,'y'=4] {'y'}, dimensions={0} | all-to-all | bytes 589824 | tf_op jit(solution)/shard_map/all_to_all | solution.py:344
  68.7 19.9 %all_to_all.112 = f32[16,48,128]{2,1,0:T(8,128)S(1)} all-to-all(f32[16,48,128]{2,1,0:T(8,128)S(1)} %pad_maximum_fusion), channel_id=1, replica_groups=mesh['x'=4,'zl'=4,'core'=2,'zh'=4,'y'=4] {'x','zl'}, dimensions={0} | all-to-all | bytes 786432 | tf_op jit(solution)/shard_map/all_to_all | solution.py:344
  88.6 0.8 slice-done
  90.2 3.5 all-to-all-start.4
  93.7 19.0 %all-to-all-done.4 = f32[4,176,128]{2,1,0:T(8,128)S(1)} async-done(((f32[4,176,128]{2,1,0:T(8,128)}), f32[4,176,128]{2,1,0:T(8,128)S(1)}, u32[]{:S(2)}, u32[]{:S(2)}) %all-to-all-start.4) | async-done | bytes 360480 | tf_op jit(solution)/shard_map/all_to_all | solution.py:344
  113.4 4.5 all-to-all-start.5
  118.0 9.7 %all-gather = f32[576,128]{1,0:T(8,128)S(1)} all-gather(f32[144,128]{1,0:T(8,128)S(1)} %pad_maximum_fusion.14), channel_id=2, replica_groups=mesh['x'=4,'zl'=4,'core'=2,'zh'=4,'y'=4] {'y'}, dimensions={0}, use_global_device_ids=true | all-gather | bytes 368640 | tf_op jit(solution)/shard_map/all_gather | solution.py:367
  127.7 9.7 %all-gather.1 = f32[1152,128]{1,0:T(8,128)S(1)} all-gather(f32[576,128]{1,0:T(8,128)S(1)} %pad_maximum_fusion.5), channel_id=3, replica_groups=mesh['x'=4,'zl'=4,'core'=2,'zh'=4,'y'=4] {'core'}, dimensions={0}, use_global_device_ids=true | all-gather | bytes 884736 | tf_op jit(solution)/shard_map/all_gather | solution.py:369
  137.4 8.0 %shard_map.68 = (f32[24,64,128]{2,1,0:T(8,128)}, f32[24,64,128]{2,1,0:T(8,128)}, f32[24,64,128]{2,1,0:T(8,128)}, f32[16,32,128]{2,1,0:T(8,128)S(1)}, f32[16,32,1...) custom-call(s32[3]{0:T(128)S(1)} %pad_add_fusion.where_ref.refs_0_, s32[4]{0:T(128)S(1)} %bitcast.60, ...), custom_call_target="tpu_custom_call", output_to_operand_aliasing={{0}: (6, {})} | custom-call | tf_op jit(solution)/shard_map/pallas_call | solution.py:398
  145.5 2.3 collective-permute-start.1
  147.8 8.9 %all_to_all.113 = f32[4,144,128]{2,1,0:T(8,128)S(1)} all-to-all(f32[4,144,128]{2,1,0:T(8,128)S(1)} %get-tuple-element.50), channel_id=1, replica_groups=mesh['x'=4,'zl'=4,'core'=2,'zh'=4,'y'=4] {'y'}, dimensions={0} | all-to-all | bytes 589824 | tf_op jit(solution)/shard_map/all_to_all | solution.py:344
  156.8 19.6 %all_to_all.114 = f32[16,48,128]{2,1,0:T(8,128)S(1)} all-to-all(f32[16,48,128]{2,1,0:T(8,128)S(1)} %pad_maximum_fusion.1), channel_id=1, replica_groups=mesh['x'=4,'zl'=4,'core'=2,'zh'=4,'y'=4] {'x','zl'}, dimensions={0} | all-to-all | bytes 786432 | tf_op jit(solution)/shard_map/all_to_all | solution.py:344
  176.4 0.8 slice-done.1
  177.3 24.9 %all_to_all.115 = f32[4,176,128]{2,1,0:T(8,128)S(1)} all-to-all(f32[4,176,128]{2,1,0:T(8,128)S(1)} %broadcast_in_dim.49), channel_id=1, replica_groups=mesh['x'=4,'zl'=4,'core'=2,'zh'=4,'y'=4] {'zh'}, dimensions={0} | all-to-all | bytes 720896 | tf_op jit(solution)/shard_map/all_to_all | solution.py:344
  203.0 3.5 all-to-all-start.9
  206.5 10.1 %all-gather.2 = f32[576,128]{1,0:T(8,128)S(1)} all-gather(f32[144,128]{1,0:T(8,128)S(1)} %pad_maximum_fusion.15), channel_id=4, replica_groups=mesh['x'=4,'zl'=4,'core'=2,'zh'=4,'y'=4] {'y'}, dimensions={0}, use_global_device_ids=true | all-gather | bytes 368640 | tf_op jit(solution)/shard_map/all_gather | solution.py:367
  216.6 9.0 %all-gather.3 = f32[1152,128]{1,0:T(8,128)S(1)} all-gather(f32[576,128]{1,0:T(8,128)S(1)} %pad_maximum_fusion.6), channel_id=5, replica_groups=mesh['x'=4,'zl'=4,'core'=2,'zh'=4,'y'=4] {'core'}, dimensions={0}, use_global_device_ids=true | all-gather | bytes 884736 | tf_op jit(solution)/shard_map/all_gather | solution.py:369
  225.6 8.6 %shard_map.69 = (f32[24,64,128]{2,1,0:T(8,128)}, f32[24,64,128]{2,1,0:T(8,128)}, f32[24,64,128]{2,1,0:T(8,128)}, f32[24,64,128]{2,1,0:T(8,128)}, f32[16,32,128]{...) custom-call(s32[3]{0:T(128)S(1)} %pad_add_fusion.where_ref.refs_0_, ...), custom_call_target="tpu_custom_call", output_to_operand_aliasing={{0}: (6, {}), {1}: (7, {}), {2}: (8, {})} | custom-call | tf_op jit(solution)/shard_map/pallas_call | solution.py:398
  234.2 2.3 collective-permute-start.2
  236.5 8.9 %all_to_all.116 = f32[4,144,128]{2,1,0:T(8,128)S(1)} all-to-all(f32[4,144,128]{2,1,0:T(8,128)S(1)} %get-tuple-element.58), channel_id=1, replica_groups=mesh['x'=4,'zl'=4,'core'=2,'zh'=4,'y'=4] {'y'}, dimensions={0} | all-to-all | bytes 589824 | tf_op jit(solution)/shard_map/all_to_all | solution.py:344
  245.6 19.5 %all_to_all.117 = f32[16,48,128]{2,1,0:T(8,128)S(1)} all-to-all(f32[16,48,128]{2,1,0:T(8,128)S(1)} %pad_maximum_fusion.2), channel_id=1, replica_groups=mesh['x'=4,'zl'=4,'core'=2,'zh'=4,'y'=4] {'x','zl'}, dimensions={0} | all-to-all | bytes 786432 | tf_op jit(solution)/shard_map/all_to_all | solution.py:344
  266.0 21.3 %all_to_all.118 = f32[4,176,128]{2,1,0:T(8,128)S(1)} all-to-all(f32[4,176,128]{2,1,0:T(8,128)S(1)} %broadcast_in_dim.53), channel_id=1, replica_groups=mesh['x'=4,'zl'=4,'core'=2,'zh'=4,'y'=4] {'zh'}, dimensions={0} | all-to-all | bytes 720896 | tf_op jit(solution)/shard_map/all_to_all | solution.py:344
  288.0 5.9 %all-to-all-start.13 = ((f32[16,32,128]{2,1,0:T(8,128)}), f32[16,32,128]{2,1,0:T(8,128)S(1)}, u32[]{:S(2)}, u32[]{:S(2)}) async-start(f32[16,32,128]{2,1,0:T(8,128)} %broadcast_in_dim.55), calls=%async_computation.13 | async-start | bytes 524288 | tf_op jit(solution)/shard_map/all_to_all | solution.py:344
  294.0 9.8 %all-gather.4 = f32[576,128]{1,0:T(8,128)S(1)} all-gather(f32[144,128]{1,0:T(8,128)S(1)} %pad_maximum_fusion.16), channel_id=6, replica_groups=mesh['x'=4,'zl'=4,'core'=2,'zh'=4,'y'=4] {'y'}, dimensions={0}, use_global_device_ids=true | all-gather | bytes 368640 | tf_op jit(solution)/shard_map/all_gather | solution.py:367
  303.8 9.1 %all-gather.5 = f32[1152,128]{1,0:T(8,128)S(1)} all-gather(f32[576,128]{1,0:T(8,128)S(1)} %pad_maximum_fusion.7), channel_id=7, replica_groups=mesh['x'=4,'zl'=4,'core'=2,'zh'=4,'y'=4] {'core'}, dimensions={0}, use_global_device_ids=true | all-gather | bytes 884736 | tf_op jit(solution)/shard_map/all_gather | solution.py:369
  312.9 8.8 %shard_map.70 = (f32[24,64,128]{2,1,0:T(8,128)}, f32[24,64,128]{2,1,0:T(8,128)}, f32[24,64,128]{2,1,0:T(8,128)}, f32[24,64,128]{2,1,0:T(8,128)}, f32[16,32,128]{...) custom-call(s32[3]{0:T(128)S(1)} %pad_add_fusion.where_ref.refs_0_, ...), custom_call_target="tpu_custom_call", output_to_operand_aliasing={{0}: (6, {}), {1}: (7, {}), {2}: (8, {}), {3}: (9, {})} | custom-call | tf_op jit(solution)/shard_map/pallas_call | solution.py:398
  321.7 2.3 collective-permute-start.3
  324.0 8.9 %all_to_all.119 = f32[4,144,128]{2,1,0:T(8,128)S(1)} all-to-all(f32[4,144,128]{2,1,0:T(8,128)S(1)} %get-tuple-element.67), channel_id=1, replica_groups=mesh['x'=4,'zl'=4,'core'=2,'zh'=4,'y'=4] {'y'}, dimensions={0} | all-to-all | bytes 589824 | tf_op jit(solution)/shard_map/all_to_all | solution.py:344
  333.1 19.6 %all_to_all.120 = f32[16,48,128]{2,1,0:T(8,128)S(1)} all-to-all(f32[16,48,128]{2,1,0:T(8,128)S(1)} %pad_maximum_fusion.3), channel_id=1, replica_groups=mesh['x'=4,'zl'=4,'core'=2,'zh'=4,'y'=4] {'x','zl'}, dimensions={0} | all-to-all | bytes 786432 | tf_op jit(solution)/shard_map/all_to_all | solution.py:344
  353.5 21.3 %all_to_all.121 = f32[4,176,128]{2,1,0:T(8,128)S(1)} all-to-all(f32[4,176,128]{2,1,0:T(8,128)S(1)} %broadcast_in_dim.57), channel_id=1, replica_groups=mesh['x'=4,'zl'=4,'core'=2,'zh'=4,'y'=4] {'zh'}, dimensions={0} | all-to-all | bytes 720896 | tf_op jit(solution)/shard_map/all_to_all | solution.py:344
  375.6 5.8 %all-to-all-start.17 = ((f32[16,32,128]{2,1,0:T(8,128)}), f32[16,32,128]{2,1,0:T(8,128)S(1)}, u32[]{:S(2)}, u32[]{:S(2)}) async-start(f32[16,32,128]{2,1,0:T(8,128)} %broadcast_in_dim.59), calls=%async_computation.17 | async-start | bytes 524288 | tf_op jit(solution)/shard_map/all_to_all | solution.py:344
  381.4 9.7 %all-gather.6 = f32[576,128]{1,0:T(8,128)S(1)} all-gather(f32[144,128]{1,0:T(8,128)S(1)} %pad_maximum_fusion.17), channel_id=8, replica_groups=mesh['x'=4,'zl'=4,'core'=2,'zh'=4,'y'=4] {'y'}, dimensions={0}, use_global_device_ids=true | all-gather | bytes 368640 | tf_op jit(solution)/shard_map/all_gather | solution.py:367
  391.2 9.2 %all-gather.7 = f32[1152,128]{1,0:T(8,128)S(1)} all-gather(f32[576,128]{1,0:T(8,128)S(1)} %pad_maximum_fusion.8), channel_id=9, replica_groups=mesh['x'=4,'zl'=4,'core'=2,'zh'=4,'y'=4] {'core'}, dimensions={0}, use_global_device_ids=true | all-gather | bytes 884736 | tf_op jit(solution)/shard_map/all_gather | solution.py:369
  400.4 8.2 %shard_map.71 = (f32[64,128]{1,0:T(8,128)S(1)}, f32[64,128]{1,0:T(8,128)S(1)}, f32[16,32,128]{2,1,0:T(8,128)S(1)}, f32[16,32,128]{2,1,0:T(8,128)S(1)}, f32[4,144,128]{2,1,0:T(8,128)S(1)}) custom-call(s32[3]{0:T(128)S(1)} %pad_add_fusion.where_ref.refs_0_, s32[4]{0:T(128)S(1)} %bitcast.63, s32[4]{0:T(128)S(1)} %bitcast.68, f32[4,128,128]{2,1,0:T(8,128)S(1)} %bitcast.46, ...), custom_call_target="tpu_custom_call" | custom-call | tf_op jit(solution)/shard_map/pallas_call | solution.py:398
  408.6 2.3 collective-permute-start.4
  410.9 8.9 %all_to_all.122 = f32[4,144,128]{2,1,0:T(8,128)S(1)} all-to-all(f32[4,144,128]{2,1,0:T(8,128)S(1)} %get-tuple-element.76), channel_id=1, replica_groups=mesh['x'=4,'zl'=4,'core'=2,'zh'=4,'y'=4] {'y'}, dimensions={0} | all-to-all | bytes 589824 | tf_op jit(solution)/shard_map/all_to_all | solution.py:344
  420.0 19.8 %all_to_all.123 = f32[16,48,128]{2,1,0:T(8,128)S(1)} all-to-all(f32[16,48,128]{2,1,0:T(8,128)S(1)} %pad_maximum_fusion.4), channel_id=1, replica_groups=mesh['x'=4,'zl'=4,'core'=2,'zh'=4,'y'=4] {'x','zl'}, dimensions={0} | all-to-all | bytes 786432 | tf_op jit(solution)/shard_map/all_to_all | solution.py:344
  440.6 14.3 %all_to_all.124 = f32[4,48,128]{2,1,0:T(8,128)S(1)} all-to-all(f32[4,48,128]{2,1,0:T(8,128)S(1)} %pad_maximum_fusion.9), channel_id=1, replica_groups=mesh['x'=4,'zl'=4,'core'=2,'zh'=4,'y'=4] {'zh'}, dimensions={0} | all-to-all | bytes 196608 | tf_op jit(solution)/shard_map/all_to_all | solution.py:344
  455.6 3.3 all-to-all-start.21
  458.9 4.3 all-to-all-done.21
  463.2 5.8 %all_gather.75.recv_ref = f32[2,64,128]{2,1,0:T(8,128)S(1)} all-gather(f32[1,64,128]{2,1,0:T(8,128)S(1)} %bitcast.84), channel_id=1, replica_groups=mesh['x'=4,'zl'=4,'core'=2,'zh'=4,'y'=4] {'core'}, dimensions={0}, use_global_device_ids=true | all-gather | bytes 98304 | tf_op jit(solution)/shard_map/all_gather | solution.py:377
  469.0 3.9 shard_map.72
  (116 shorter events, 10.1 us)
Async XLA Ops:
  30.1 15.8 %all-to-all-start = ((f32[16,32,128]{2,1,0:T(8,128)}), f32[16,32,128]{2,1,0:T(8,128)S(1)}, u32[]{:S(2)}, u32[]{:S(2)}) async-start(f32[16,32,128]{2,1,0:T(8,128)} %broadcast_in_dim.42), calls=%async_computation | async-start | bytes 524288 | tf_op jit(solution)/shard_map/all_to_all | solution.py:344
  45.9 7.1 %copy-start = (f32[1,1,4,128,128]{4,3,2,1,0:T(8,128)S(1)}, f32[1,1,4,128,128]{4,3,2,1,0:T(8,128)}, u32[]{:S(2)}) copy-start(f32[1,1,4,128,128]{4,3,2,1,0:T(8,128)} %param.5) | copy-start | bytes 786436
  53.0 0.7 copy-start.1
  53.0 0.7 copy-start.2
  56.5 12.1 %collective-permute-start = (f32[16,32,128]{2,1,0:T(8,128)S(1)}, f32[16,32,128]{2,1,0:T(8,128)S(1)}, u32[]{:S(2)}, u32[]{:S(2)}) collective-permute-start(f32[16,32,128]{2,1,0:T(8,128)S(1)} %get-tuple-element.43), channel_id=1, source_target_pairs={{0,16},{16,0},{1,17},{17,1},{2,18},{18,2},{3,19},{19,3},{4,20},{20... | collective-permute-start | bytes 786440 | tf_op jit(solution)/shard_map/ppermute | solution.py:350
  68.6 20.0 %copy-start.3 = (f32[144,128]{1,0:T(8,128)}, f32[144,128]{1,0:T(8,128)S(1)}, u32[]{:S(2)}) copy-start(f32[144,128]{1,0:T(8,128)S(1)} %reduce_sum.171) | copy-start | bytes 221188
  88.6 0.8 slice-start
  90.2 22.4 %all-to-all-start.4 = ((f32[4,176,128]{2,1,0:T(8,128)}), f32[4,176,128]{2,1,0:T(8,128)S(1)}, u32[]{:S(2)}, u32[]{:S(2)}) async-start(f32[4,176,128]{2,1,0:T(8,128)} %broadcast_in_dim.45), calls=%async_computation.4 | async-start | bytes 720896 | tf_op jit(solution)/shard_map/all_to_all | solution.py:344
  113.4 14.3 %all-to-all-start.5 = ((f32[16,32,128]{2,1,0:T(8,128)}), f32[16,32,128]{2,1,0:T(8,128)S(1)}, u32[]{:S(2)}, u32[]{:S(2)}) async-start(f32[16,32,128]{2,1,0:T(8,128)} %broadcast_in_dim.47), calls=%async_computation.5 | async-start | bytes 524288 | tf_op jit(solution)/shard_map/all_to_all | solution.py:344
  145.5 11.3 %collective-permute-start.1 = (f32[16,32,128]{2,1,0:T(8,128)S(1)}, f32[16,32,128]{2,1,0:T(8,128)S(1)}, u32[]{:S(2)}, u32[]{:S(2)}) collective-permute-start(f32[16,32,128]{2,1,0:T(8,128)S(1)} %get-tuple-element.49), channel_id=1, source_target_pairs={{0,16},{16,0},{1,17},{17,1},{2,18},{18,2},{3,19},{19,3},{4,20},{20... | collective-permute-start | bytes 786440 | tf_op jit(solution)/shard_map/ppermute | solution.py:350
  156.7 19.7 %copy-start.4 = (f32[144,128]{1,0:T(8,128)}, f32[144,128]{1,0:T(8,128)S(1)}, u32[]{:S(2)}) copy-start(f32[144,128]{1,0:T(8,128)S(1)} %reduce_sum.175) | copy-start | bytes 221188
  176.4 0.8 slice-start.1
  203.0 13.6 %all-to-all-start.9 = ((f32[16,32,128]{2,1,0:T(8,128)}), f32[16,32,128]{2,1,0:T(8,128)S(1)}, u32[]{:S(2)}, u32[]{:S(2)}) async-start(f32[16,32,128]{2,1,0:T(8,128)} %broadcast_in_dim.51), calls=%async_computation.9 | async-start | bytes 524288 | tf_op jit(solution)/shard_map/all_to_all | solution.py:344
  234.2 11.3 %collective-permute-start.2 = (f32[16,32,128]{2,1,0:T(8,128)S(1)}, f32[16,32,128]{2,1,0:T(8,128)S(1)}, u32[]{:S(2)}, u32[]{:S(2)}) collective-permute-start(f32[16,32,128]{2,1,0:T(8,128)S(1)} %get-tuple-element.57), channel_id=1, source_target_pairs={{0,16},{16,0},{1,17},{17,1},{2,18},{18,2},{3,19},{19,3},{4,20},{20... | collective-permute-start | bytes 786440 | tf_op jit(solution)/shard_map/ppermute | solution.py:350
  245.5 19.6 %copy-start.5 = (f32[144,128]{1,0:T(8,128)}, f32[144,128]{1,0:T(8,128)S(1)}, u32[]{:S(2)}) copy-start(f32[144,128]{1,0:T(8,128)S(1)} %reduce_sum.179) | copy-start | bytes 221188
  265.1 0.8 slice-start.2
  288.0 15.7 %all-to-all-start.13 = ((f32[16,32,128]{2,1,0:T(8,128)}), f32[16,32,128]{2,1,0:T(8,128)S(1)}, u32[]{:S(2)}, u32[]{:S(2)}) async-start(f32[16,32,128]{2,1,0:T(8,128)} %broadcast_in_dim.55), calls=%async_computation.13 | async-start | bytes 524288 | tf_op jit(solution)/shard_map/all_to_all | solution.py:344
  321.7 11.3 %collective-permute-start.3 = (f32[16,32,128]{2,1,0:T(8,128)S(1)}, f32[16,32,128]{2,1,0:T(8,128)S(1)}, u32[]{:S(2)}, u32[]{:S(2)}) collective-permute-start(f32[16,32,128]{2,1,0:T(8,128)S(1)} %get-tuple-element.66), channel_id=1, source_target_pairs={{0,16},{16,0},{1,17},{17,1},{2,18},{18,2},{3,19},{19,3},{4,20},{20... | collective-permute-start | bytes 786440 | tf_op jit(solution)/shard_map/ppermute | solution.py:350
  333.0 19.7 %copy-start.6 = (f32[144,128]{1,0:T(8,128)}, f32[144,128]{1,0:T(8,128)S(1)}, u32[]{:S(2)}) copy-start(f32[144,128]{1,0:T(8,128)S(1)} %reduce_sum.183) | copy-start | bytes 221188
  352.7 0.8 slice-start.3
  375.6 15.6 %all-to-all-start.17 = ((f32[16,32,128]{2,1,0:T(8,128)}), f32[16,32,128]{2,1,0:T(8,128)S(1)}, u32[]{:S(2)}, u32[]{:S(2)}) async-start(f32[16,32,128]{2,1,0:T(8,128)} %broadcast_in_dim.59), calls=%async_computation.17 | async-start | bytes 524288 | tf_op jit(solution)/shard_map/all_to_all | solution.py:344
  408.6 11.3 %collective-permute-start.4 = (f32[16,32,128]{2,1,0:T(8,128)S(1)}, f32[16,32,128]{2,1,0:T(8,128)S(1)}, u32[]{:S(2)}, u32[]{:S(2)}) collective-permute-start(f32[16,32,128]{2,1,0:T(8,128)S(1)} %get-tuple-element.75), channel_id=1, source_target_pairs={{0,16},{16,0},{1,17},{17,1},{2,18},{18,2},{3,19},{19,3},{4,20},{20... | collective-permute-start | bytes 786440 | tf_op jit(solution)/shard_map/ppermute | solution.py:350
  419.8 20.0 %copy-start.7 = (f32[144,128]{1,0:T(8,128)}, f32[144,128]{1,0:T(8,128)S(1)}, u32[]{:S(2)}) copy-start(f32[144,128]{1,0:T(8,128)S(1)} %reduce_sum.187) | copy-start | bytes 221188
  439.8 0.8 slice-start.4
  455.6 7.5 %all-to-all-start.21 = ((f32[4,16,128]{2,1,0:T(8,128)}), f32[4,16,128]{2,1,0:T(8,128)S(1)}, u32[]{:S(2)}, u32[]{:S(2)}) async-start(f32[4,16,128]{2,1,0:T(8,128)} %broadcast_in_dim.62), calls=%async_computation.21 | async-start | bytes 65536 | tf_op jit(solution)/shard_map/all_to_all | solution.py:344

commit v2 on v1

--- a/solution.py
+++ b/solution.py
@@ -178,7 +178,7 @@
             send_y_ref[y, zh * (VEC // 2) : (zh + 1) * (VEC // 2), :] = block
 
 
-def unpack_gathered(recv_row_ref, recv_col_ref, n_row, n_col, out):
+def unpack_gathered(recv_row_ref, recv_col_ref, n_row, n_col, out, by_chip=False):
     n_y = recv_col_ref.shape[0]
     half = VEC // 2
 
@@ -191,7 +191,11 @@
         out[s, :half, :] = top
         out[s, half:, :] = bottom
     for b in range(n_row // 2):
-        top, bottom = unpack_pair(*(recv_row_ref[core, b * half : (b + 1) * half, :] for core in range(2)))
+        if by_chip:
+            pair = [recv_row_ref[b, core * half : (core + 1) * half, :] for core in range(2)]
+        else:
+            pair = [recv_row_ref[core, b * half : (b + 1) * half, :] for core in range(2)]
+        top, bottom = unpack_pair(*pair)
         out[n_col // 2 + b, :half, :] = top
         out[n_col // 2 + b, half:, :] = bottom
 
@@ -204,7 +208,7 @@
     n_row, n_col, where_ref, rows_ref, cols_ref, tiles_ref, recv_row_ref, recv_col_ref,
     trial_ref, keep_ref, give_ref, send_y_ref, fresh, direct, mirrored, sem,
 ):
-    unpack_gathered(recv_row_ref, recv_col_ref, n_row, n_col, fresh)
+    unpack_gathered(recv_row_ref, recv_col_ref, n_row, n_col, fresh, by_chip=True)
     store = pltpu.make_async_copy(fresh, trial_ref, sem)
     store.start()
 
@@ -348,11 +352,12 @@
 
     def reduce_row_and_y(keep, give, y_blocks):
         both_cores = keep + lax.ppermute(give, "core", [(0, 1), (1, 0)])
-        along_y = jnp.sum(exchange(y_blocks, "y"), axis=0)
-        sums = jnp.broadcast_to(along_y[None, n_direct:], (n_row // 2, sums_rows, TILE))
+        from_y = exchange(y_blocks, "y")
+        sums = jnp.sum(from_y[:, n_direct:], axis=0)
+        sums = jnp.broadcast_to(sums[None], (n_row // 2, sums_rows, TILE))
         from_chips = exchange(jnp.concatenate([both_cores, sums], axis=1), CHIPS)
-        from_chips, along_y = lax.optimization_barrier((from_chips, along_y))
-        return jnp.sum(from_chips, axis=0), along_y[:n_direct]
+        from_chips, from_y = lax.optimization_barrier((from_chips, from_y))
+        return jnp.sum(from_chips, axis=0), jnp.sum(from_y[:, :n_direct], axis=0)
 
     def gather_chips(block):
         return spread(block, CHIPS, n_row // 2).reshape(n_row // 2 * half, TILE)
@@ -378,9 +383,9 @@
 
     start = jnp.concatenate([initial_block[:half], initial_block[half:]], axis=1)
     along_z = spread(start, "zh", n_zh)
-    from_chips = gather_chips(start)
+    both_cores = lax.all_gather(start, "core", axis=0, tiled=True)
+    from_row = spread(both_cores, CHIPS, n_row // 2)
     from_col = lax.all_gather(along_z.reshape(n_direct, TILE), "y", axis=0)
-    from_row = lax.all_gather(from_chips, "core", axis=0)
     trial, *messages = pl.pallas_call(
         functools.partial(first_kernel, n_row, n_col),
         out_shape=(state,) + sends,

time: 475 us -> 463 us (0.975)
  blocking collectives: 353 us -> 274 us
  starting transfers between devices: 43.4 us -> 82.1 us
  waiting for transfers between devices: 23.3 us -> 51.2 us
    all_to_all x15 -> x9, blocking collectives: 253 us -> 170 us  [exchange(): return lax.all_to_all(blocks, axes, 0, 0, tiled=True)]
    all_to_all x7 -> x13, starting transfers between devices: 31.9 us -> 68.7 us  [exchange(): return lax.all_to_all(blocks, axes, 0, 0, tiled=True)]
    all_to_all x7 -> x13, waiting for transfers between devices: 23.2 us -> 51.2 us  [exchange(): return lax.all_to_all(blocks, axes, 0, 0, tiled=True)]
    all_gather x4, blocking collectives: 39.4 us -> 46.8 us  [apply_and_gather(): lax.all_gather(jnp.concatenate([blocks.reshape(n_direct, TILE), sums], ax...]
  transfers between devices with their start and end apart: 12 -> 18, of which waited for: 2 -> 9; matrix products, arithmetic and copies ran while one was open for 0% -> 0% of each run, Pallas kernels for 0% -> 0%
where the time goes in v2:
time: 463 us; the launch traced here: 461 us
  blocking collectives  274 us (59%)
  starting transfers between devices  82.1 us (18%)
  waiting for transfers between devices  51.2 us (11%)
  Pallas kernels  44 us (10%)
  local copies, waits for them, and re-layouts  7.37 us (2%)
    all_to_all x9, blocking collectives, exchange(): return lax.all_to_all(blocks, axes, 0, 0, tiled=True)  170 us
    all_to_all x13, starting transfers between devices, exchange(): return lax.all_to_all(blocks, axes, 0, 0, tiled=True)  68.7 us
    all_to_all x13, waiting for transfers between devices, exchange(): return lax.all_to_all(blocks, axes, 0, 0, tiled=True)  51.2 us
    all_gather x4, blocking collectives, apply_and_gather(): lax.all_gather(jnp.concatenate([blocks.reshape(n_direct, TILE), sums], ax...  46.8 us
    all_gather x4, blocking collectives, apply_and_gather(): lax.all_gather(jnp.concatenate([from_chips, sums], axis=0), 'core', axis=0)  37.9 us
    pallas_call x4, Pallas kernels, per_device(): pl.pallas_call(functools.partial(middle_kernel, step, n_row, n_col), out_...  36.4 us
    ppermute x5, starting transfers between devices, reduce_row_and_y(): both_cores = keep + lax.ppermute(give, 'core', [(0, 1), (1, 0)])  13.4 us
    all_gather x1, blocking collectives, per_device(): from_col = lax.all_gather(along_z.reshape(n_direct, TILE), 'y', axis=0)  10.2 us
  transfers between devices with their start and end apart: 18, of which 9 were waited for; matrix products, arithmetic and copies ran while one was open for 0% of the time, Pallas kernels for 0%

profile of v2, /device:TPU:1, one launch (start us, length us, event | category | flops | bytes accessed | tf_op | source)
XLA Modules:
  0.0 461.3 jit_solution(5703388192118472)
XLA Ops:
  2.1 15.6 %all-to-all-start.1 = ((f32[4,32,128]{2,1,0:T(8,128)}), f32[4,32,128]{2,1,0:T(8,128)S(1)}, u32[]{:S(2)}, u32[]{:S(2)}) async-start(f32[4,32,128]{2,1,0:T(8,128)} %broadcast_in_dim.43), calls=%async_computation.1 | async-start | bytes 131072 | tf_op jit(solution)/shard_map/all_to_all | solution.py:348
  17.7 2.4 all_gather.57
  20.1 10.1 %all-to-all-done.1 = f32[4,32,128]{2,1,0:T(8,128)S(1)} async-done(((f32[4,32,128]{2,1,0:T(8,128)}), f32[4,32,128]{2,1,0:T(8,128)S(1)}, u32[]{:S(2)}, u32[]{:S(2)}) %all-to-all-start.1) | async-done | bytes 65568 | tf_op jit(solution)/shard_map/all_to_all | solution.py:348
  31.1 5.5 %all-to-all-start = ((f32[16,64,128]{2,1,0:T(8,128)}), f32[16,64,128]{2,1,0:T(8,128)S(1)}, u32[]{:S(2)}, u32[]{:S(2)}) async-start(f32[16,64,128]{2,1,0:T(8,128)} %broadcast_in_dim.42), calls=%async_computation | async-start | bytes 1048576 | tf_op jit(solution)/shard_map/all_to_all | solution.py:348
  36.7 10.2 %all_gather.58.recv_col_ref = f32[4,128,128]{2,1,0:T(8,128)S(1)} all-gather(f32[1,128,128]{2,1,0:T(8,128)S(1)} %bitcast.81), channel_id=1, replica_groups=mesh['x'=4,'zl'=4,'core'=2,'zh'=4,'y'=4] {'y'}, dimensions={0}, use_global_device_ids=true | all-gather | bytes 327680 | tf_op jit(solution)/shard_map/all_gather | solution.py:388
  46.9 5.1 %all-to-all-done.recv_row_ref = f32[16,64,128]{2,1,0:T(8,128)S(1)} async-done(((f32[16,64,128]{2,1,0:T(8,128)}), f32[16,64,128]{2,1,0:T(8,128)S(1)}, u32[]{:S(2)}, u32[]{:S(2)}) %all-to-all-start) | async-done | bytes 524320 | tf_op jit(solution)/shard_map/all_to_all | solution.py:348
  52.6 3.7 shard_map.67
  56.4 4.2 all-to-all-start.2
  60.6 4.2 collective-permute-start
  66.4 13.5 %all_to_all.110 = f32[16,48,128]{2,1,0:T(8,128)S(1)} all-to-all(f32[16,48,128]{2,1,0:T(8,128)S(1)} %pad_maximum_fusion), channel_id=1, replica_groups=mesh['x'=4,'zl'=4,'core'=2,'zh'=4,'y'=4] {'x','zl'}, dimensions={0} | all-to-all | bytes 786432 | tf_op jit(solution)/shard_map/all_to_all | solution.py:348
  80.7 3.5 all-to-all-start.4
  84.1 13.7 %all-to-all-done.4 = f32[4,176,128]{2,1,0:T(8,128)S(1)} async-done(((f32[4,176,128]{2,1,0:T(8,128)}), f32[4,176,128]{2,1,0:T(8,128)S(1)}, u32[]{:S(2)}, u32[]{:S(2)}) %all-to-all-start.4) | async-done | bytes 360480 | tf_op jit(solution)/shard_map/all_to_all | solution.py:348
  98.7 5.9 %all-to-all-start.5 = ((f32[16,32,128]{2,1,0:T(8,128)}), f32[16,32,128]{2,1,0:T(8,128)S(1)}, u32[]{:S(2)}, u32[]{:S(2)}) async-start(f32[16,32,128]{2,1,0:T(8,128)} %broadcast_in_dim.47), calls=%async_computation.5 | async-start | bytes 524288 | tf_op jit(solution)/shard_map/all_to_all | solution.py:348
  104.6 17.6 %all-gather = f32[576,128]{1,0:T(8,128)S(1)} all-gather(f32[144,128]{1,0:T(8,128)S(1)} %pad_maximum_fusion.14), channel_id=2, replica_groups=mesh['x'=4,'zl'=4,'core'=2,'zh'=4,'y'=4] {'y'}, dimensions={0}, use_global_device_ids=true | all-gather | bytes 368640 | tf_op jit(solution)/shard_map/all_gather | solution.py:372
  122.2 9.7 %all-gather.1 = f32[1152,128]{1,0:T(8,128)S(1)} all-gather(f32[576,128]{1,0:T(8,128)S(1)} %pad_maximum_fusion.5), channel_id=3, replica_groups=mesh['x'=4,'zl'=4,'core'=2,'zh'=4,'y'=4] {'core'}, dimensions={0}, use_global_device_ids=true | all-gather | bytes 884736 | tf_op jit(solution)/shard_map/all_gather | solution.py:374
  131.9 8.7 %shard_map.68 = (f32[24,64,128]{2,1,0:T(8,128)}, f32[24,64,128]{2,1,0:T(8,128)}, f32[24,64,128]{2,1,0:T(8,128)}, f32[16,32,128]{2,1,0:T(8,128)S(1)}, f32[16,32,128]{2,1,0:T(8,128)S(1)}, /*index=5*/f32[4,144,128]{2,1,0:T(8,128)}) custom-call(s32[3]{0:T(128)S(1)} %pad_add_fusion.where_ref.refs_0_, s32[4]{0:T(128)S(1)} %bitcast.59, ...), custom_call_target="tpu_custom_call", output_to_operand_aliasing={{0}: (6, {})} | custom-call | tf_op jit(solution)/shard_map/pallas_call | solution.py:403
  140.6 3.5 all-to-all-start.6
  146.4 4.1 all-to-all-done.6
  150.6 19.5 %all_to_all.111 = f32[16,48,128]{2,1,0:T(8,128)S(1)} all-to-all(f32[16,48,128]{2,1,0:T(8,128)S(1)} %pad_maximum_fusion.1), channel_id=1, replica_groups=mesh['x'=4,'zl'=4,'core'=2,'zh'=4,'y'=4] {'x','zl'}, dimensions={0} | all-to-all | bytes 786432 | tf_op jit(solution)/shard_map/all_to_all | solution.py:348
  170.2 22.0 %all_to_all.112 = f32[4,176,128]{2,1,0:T(8,128)S(1)} all-to-all(f32[4,176,128]{2,1,0:T(8,128)S(1)} %broadcast_in_dim.49), channel_id=1, replica_groups=mesh['x'=4,'zl'=4,'core'=2,'zh'=4,'y'=4] {'zh'}, dimensions={0} | all-to-all | bytes 720896 | tf_op jit(solution)/shard_map/all_to_all | solution.py:348
  193.0 5.4 %all-to-all-start.9 = ((f32[16,32,128]{2,1,0:T(8,128)}), f32[16,32,128]{2,1,0:T(8,128)S(1)}, u32[]{:S(2)}, u32[]{:S(2)}) async-start(f32[16,32,128]{2,1,0:T(8,128)} %broadcast_in_dim.51), calls=%async_computation.9 | async-start | bytes 524288 | tf_op jit(solution)/shard_map/all_to_all | solution.py:348
  198.5 9.7 %all-gather.2 = f32[576,128]{1,0:T(8,128)S(1)} all-gather(f32[144,128]{1,0:T(8,128)S(1)} %pad_maximum_fusion.15), channel_id=4, replica_groups=mesh['x'=4,'zl'=4,'core'=2,'zh'=4,'y'=4] {'y'}, dimensions={0}, use_global_device_ids=true | all-gather | bytes 368640 | tf_op jit(solution)/shard_map/all_gather | solution.py:372
  208.3 9.8 %all-gather.3 = f32[1152,128]{1,0:T(8,128)S(1)} all-gather(f32[576,128]{1,0:T(8,128)S(1)} %pad_maximum_fusion.6), channel_id=5, replica_groups=mesh['x'=4,'zl'=4,'core'=2,'zh'=4,'y'=4] {'core'}, dimensions={0}, use_global_device_ids=true | all-gather | bytes 884736 | tf_op jit(solution)/shard_map/all_gather | solution.py:374
  218.0 9.5 %shard_map.69 = (f32[24,64,128]{2,1,0:T(8,128)}, f32[24,64,128]{2,1,0:T(8,128)}, f32[24,64,128]{2,1,0:T(8,128)}, f32[24,64,128]{2,1,0:T(8,128)}, f32[16,32,128]{...) custom-call(s32[3]{0:T(128)S(1)} %pad_add_fusion.where_ref.refs_0_, ...), custom_call_target="tpu_custom_call", output_to_operand_aliasing={{0}: (6, {}), {1}: (7, {}), {2}: (8, {})} | custom-call | tf_op jit(solution)/shard_map/pallas_call | solution.py:403
  227.6 3.5 all-to-all-start.10
  233.3 4.2 all-to-all-done.10
  237.6 19.5 %all_to_all.113 = f32[16,48,128]{2,1,0:T(8,128)S(1)} all-to-all(f32[16,48,128]{2,1,0:T(8,128)S(1)} %pad_maximum_fusion.2), channel_id=1, replica_groups=mesh['x'=4,'zl'=4,'core'=2,'zh'=4,'y'=4] {'x','zl'}, dimensions={0} | all-to-all | bytes 786432 | tf_op jit(solution)/shard_map/all_to_all | solution.py:348
  257.2 21.3 %all_to_all.114 = f32[4,176,128]{2,1,0:T(8,128)S(1)} all-to-all(f32[4,176,128]{2,1,0:T(8,128)S(1)} %broadcast_in_dim.53), channel_id=1, replica_groups=mesh['x'=4,'zl'=4,'core'=2,'zh'=4,'y'=4] {'zh'}, dimensions={0} | all-to-all | bytes 720896 | tf_op jit(solution)/shard_map/all_to_all | solution.py:348
  279.3 5.8 %all-to-all-start.13 = ((f32[16,32,128]{2,1,0:T(8,128)}), f32[16,32,128]{2,1,0:T(8,128)S(1)}, u32[]{:S(2)}, u32[]{:S(2)}) async-start(f32[16,32,128]{2,1,0:T(8,128)} %broadcast_in_dim.55), calls=%async_computation.13 | async-start | bytes 524288 | tf_op jit(solution)/shard_map/all_to_all | solution.py:348
  285.0 9.7 %all-gather.4 = f32[576,128]{1,0:T(8,128)S(1)} all-gather(f32[144,128]{1,0:T(8,128)S(1)} %pad_maximum_fusion.16), channel_id=6, replica_groups=mesh['x'=4,'zl'=4,'core'=2,'zh'=4,'y'=4] {'y'}, dimensions={0}, use_global_device_ids=true | all-gather | bytes 368640 | tf_op jit(solution)/shard_map/all_gather | solution.py:372
  294.8 9.3 %all-gather.5 = f32[1152,128]{1,0:T(8,128)S(1)} all-gather(f32[576,128]{1,0:T(8,128)S(1)} %pad_maximum_fusion.7), channel_id=7, replica_groups=mesh['x'=4,'zl'=4,'core'=2,'zh'=4,'y'=4] {'core'}, dimensions={0}, use_global_device_ids=true | all-gather | bytes 884736 | tf_op jit(solution)/shard_map/all_gather | solution.py:374
  304.1 9.2 %shard_map.70 = (f32[24,64,128]{2,1,0:T(8,128)}, f32[24,64,128]{2,1,0:T(8,128)}, f32[24,64,128]{2,1,0:T(8,128)}, f32[24,64,128]{2,1,0:T(8,128)}, f32[16,32,128]{...) custom-call(s32[3]{0:T(128)S(1)} %pad_add_fusion.where_ref.refs_0_, ...), custom_call_target="tpu_custom_call", output_to_operand_aliasing={{0}: (6, {}), {1}: (7, {}), {2}: (8, {}), {3}: (9, {})} | custom-call | tf_op jit(solution)/shard_map/pallas_call | solution.py:403
  313.3 3.5 all-to-all-start.14
  319.1 4.2 all-to-all-done.14
  323.3 19.5 %all_to_all.115 = f32[16,48,128]{2,1,0:T(8,128)S(1)} all-to-all(f32[16,48,128]{2,1,0:T(8,128)S(1)} %pad_maximum_fusion.3), channel_id=1, replica_groups=mesh['x'=4,'zl'=4,'core'=2,'zh'=4,'y'=4] {'x','zl'}, dimensions={0} | all-to-all | bytes 786432 | tf_op jit(solution)/shard_map/all_to_all | solution.py:348
  342.9 21.5 %all_to_all.116 = f32[4,176,128]{2,1,0:T(8,128)S(1)} all-to-all(f32[4,176,128]{2,1,0:T(8,128)S(1)} %broadcast_in_dim.57), channel_id=1, replica_groups=mesh['x'=4,'zl'=4,'core'=2,'zh'=4,'y'=4] {'zh'}, dimensions={0} | all-to-all | bytes 720896 | tf_op jit(solution)/shard_map/all_to_all | solution.py:348
  365.2 5.8 %all-to-all-start.17 = ((f32[16,32,128]{2,1,0:T(8,128)}), f32[16,32,128]{2,1,0:T(8,128)S(1)}, u32[]{:S(2)}, u32[]{:S(2)}) async-start(f32[16,32,128]{2,1,0:T(8,128)} %broadcast_in_dim.59), calls=%async_computation.17 | async-start | bytes 524288 | tf_op jit(solution)/shard_map/all_to_all | solution.py:348
  371.1 9.7 %all-gather.6 = f32[576,128]{1,0:T(8,128)S(1)} all-gather(f32[144,128]{1,0:T(8,128)S(1)} %pad_maximum_fusion.17), channel_id=8, replica_groups=mesh['x'=4,'zl'=4,'core'=2,'zh'=4,'y'=4] {'y'}, dimensions={0}, use_global_device_ids=true | all-gather | bytes 368640 | tf_op jit(solution)/shard_map/all_gather | solution.py:372
  380.8 9.2 %all-gather.7 = f32[1152,128]{1,0:T(8,128)S(1)} all-gather(f32[576,128]{1,0:T(8,128)S(1)} %pad_maximum_fusion.8), channel_id=9, replica_groups=mesh['x'=4,'zl'=4,'core'=2,'zh'=4,'y'=4] {'core'}, dimensions={0}, use_global_device_ids=true | all-gather | bytes 884736 | tf_op jit(solution)/shard_map/all_gather | solution.py:374
  390.0 8.9 %shard_map.71 = (f32[64,128]{1,0:T(8,128)S(1)}, f32[64,128]{1,0:T(8,128)S(1)}, f32[16,32,128]{2,1,0:T(8,128)S(1)}, f32[16,32,128]{2,1,0:T(8,128)S(1)}, f32[4,144,128]{2,1,0:T(8,128)}) custom-call(s32[3]{0:T(128)S(1)} %pad_add_fusion.where_ref.refs_0_, s32[4]{0:T(128)S(1)} %bitcast.62, s32[4]{0:T(128)S(1)} %bitcast.67, f32[4,128,128]{2,1,0:T(8,128)S(1)} %bitcast.45, ...), custom_call_target="tpu_custom_call" | custom-call | tf_op jit(solution)/shard_map/pallas_call | solution.py:403
  399.0 3.5 all-to-all-start.18
  404.8 4.1 all-to-all-done.18
  409.0 19.5 %all_to_all.117 = f32[16,48,128]{2,1,0:T(8,128)S(1)} all-to-all(f32[16,48,128]{2,1,0:T(8,128)S(1)} %pad_maximum_fusion.4), channel_id=1, replica_groups=mesh['x'=4,'zl'=4,'core'=2,'zh'=4,'y'=4] {'x','zl'}, dimensions={0} | all-to-all | bytes 786432 | tf_op jit(solution)/shard_map/all_to_all | solution.py:348
  428.6 14.2 %all_to_all.118 = f32[4,48,128]{2,1,0:T(8,128)S(1)} all-to-all(f32[4,48,128]{2,1,0:T(8,128)S(1)} %pad_maximum_fusion.9), channel_id=1, replica_groups=mesh['x'=4,'zl'=4,'core'=2,'zh'=4,'y'=4] {'zh'}, dimensions={0} | all-to-all | bytes 196608 | tf_op jit(solution)/shard_map/all_to_all | solution.py:348
  443.5 3.3 all-to-all-start.21
  446.8 4.3 all-to-all-done.21
  451.0 6.4 %all_gather.75.recv_ref = f32[2,64,128]{2,1,0:T(8,128)S(1)} all-gather(f32[1,64,128]{2,1,0:T(8,128)S(1)} %bitcast.82), channel_id=1, replica_groups=mesh['x'=4,'zl'=4,'core'=2,'zh'=4,'y'=4] {'core'}, dimensions={0}, use_global_device_ids=true | all-gather | bytes 98304 | tf_op jit(solution)/shard_map/all_gather | solution.py:382
  457.4 3.9 shard_map.72
  (102 shorter events, 19.1 us)
Async XLA Ops:
  2.1 28.1 %all-to-all-start.1 = ((f32[4,32,128]{2,1,0:T(8,128)}), f32[4,32,128]{2,1,0:T(8,128)S(1)}, u32[]{:S(2)}, u32[]{:S(2)}) async-start(f32[4,32,128]{2,1,0:T(8,128)} %broadcast_in_dim.43), calls=%async_computation.1 | async-start | bytes 131072 | tf_op jit(solution)/shard_map/all_to_all | solution.py:348
  31.1 20.9 %all-to-all-start = ((f32[16,64,128]{2,1,0:T(8,128)}), f32[16,64,128]{2,1,0:T(8,128)S(1)}, u32[]{:S(2)}, u32[]{:S(2)}) async-start(f32[16,64,128]{2,1,0:T(8,128)} %broadcast_in_dim.42), calls=%async_computation | async-start | bytes 1048576 | tf_op jit(solution)/shard_map/all_to_all | solution.py:348
  36.6 15.4 %copy-start = (f32[1,1,4,128,128]{4,3,2,1,0:T(8,128)S(1)}, f32[1,1,4,128,128]{4,3,2,1,0:T(8,128)}, u32[]{:S(2)}) copy-start(f32[1,1,4,128,128]{4,3,2,1,0:T(8,128)} %param.5) | copy-start | bytes 786436
  52.0 0.7 copy-start.1
  52.0 0.7 copy-start.2
  56.4 9.9 %all-to-all-start.2 = ((f32[4,144,128]{2,1,0:T(8,128)}), f32[4,144,128]{2,1,0:T(8,128)S(1)}, u32[]{:S(2)}, u32[]{:S(2)}) async-start(f32[4,144,128]{2,1,0:T(8,128)} %get-tuple-element.44), calls=%async_computation.2 | async-start | bytes 589824 | tf_op jit(solution)/shard_map/all_to_all | solution.py:348
  60.6 5.7 %collective-permute-start = (f32[16,32,128]{2,1,0:T(8,128)S(1)}, f32[16,32,128]{2,1,0:T(8,128)S(1)}, u32[]{:S(2)}, u32[]{:S(2)}) collective-permute-start(f32[16,32,128]{2,1,0:T(8,128)S(1)} %get-tuple-element.43), channel_id=1, source_target_pairs={{0,16},{16,0},{1,17},{17,1},{2,18},{18,2},{3,19},{19,3},{4,20},{20... | collective-permute-start | bytes 786440 | tf_op jit(solution)/shard_map/ppermute | solution.py:354
  80.7 17.2 %all-to-all-start.4 = ((f32[4,176,128]{2,1,0:T(8,128)}), f32[4,176,128]{2,1,0:T(8,128)S(1)}, u32[]{:S(2)}, u32[]{:S(2)}) async-start(f32[4,176,128]{2,1,0:T(8,128)} %broadcast_in_dim.45), calls=%async_computation.4 | async-start | bytes 720896 | tf_op jit(solution)/shard_map/all_to_all | solution.py:348
  98.7 23.5 %all-to-all-start.5 = ((f32[16,32,128]{2,1,0:T(8,128)}), f32[16,32,128]{2,1,0:T(8,128)S(1)}, u32[]{:S(2)}, u32[]{:S(2)}) async-start(f32[16,32,128]{2,1,0:T(8,128)} %broadcast_in_dim.47), calls=%async_computation.5 | async-start | bytes 524288 | tf_op jit(solution)/shard_map/all_to_all | solution.py:348
  140.6 9.9 %all-to-all-start.6 = ((f32[4,144,128]{2,1,0:T(8,128)}), f32[4,144,128]{2,1,0:T(8,128)S(1)}, u32[]{:S(2)}, u32[]{:S(2)}) async-start(f32[4,144,128]{2,1,0:T(8,128)} %get-tuple-element.50), calls=%async_computation.6 | async-start | bytes 589824 | tf_op jit(solution)/shard_map/all_to_all | solution.py:348
  144.1 6.4 %collective-permute-start.1 = (f32[16,32,128]{2,1,0:T(8,128)S(1)}, f32[16,32,128]{2,1,0:T(8,128)S(1)}, u32[]{:S(2)}, u32[]{:S(2)}) collective-permute-start(f32[16,32,128]{2,1,0:T(8,128)S(1)} %get-tuple-element.49), channel_id=1, source_target_pairs={{0,16},{16,0},{1,17},{17,1},{2,18},{18,2},{3,19},{19,3},{4,20},{20... | collective-permute-start | bytes 786440 | tf_op jit(solution)/shard_map/ppermute | solution.py:354
  193.0 15.2 %all-to-all-start.9 = ((f32[16,32,128]{2,1,0:T(8,128)}), f32[16,32,128]{2,1,0:T(8,128)S(1)}, u32[]{:S(2)}, u32[]{:S(2)}) async-start(f32[16,32,128]{2,1,0:T(8,128)} %broadcast_in_dim.51), calls=%async_computation.9 | async-start | bytes 524288 | tf_op jit(solution)/shard_map/all_to_all | solution.py:348
  227.6 9.9 %all-to-all-start.10 = ((f32[4,144,128]{2,1,0:T(8,128)}), f32[4,144,128]{2,1,0:T(8,128)S(1)}, u32[]{:S(2)}, u32[]{:S(2)}) async-start(f32[4,144,128]{2,1,0:T(8,128)} %get-tuple-element.58), calls=%async_computation.10 | async-start | bytes 589824 | tf_op jit(solution)/shard_map/all_to_all | solution.py:348
  231.0 6.5 %collective-permute-start.2 = (f32[16,32,128]{2,1,0:T(8,128)S(1)}, f32[16,32,128]{2,1,0:T(8,128)S(1)}, u32[]{:S(2)}, u32[]{:S(2)}) collective-permute-start(f32[16,32,128]{2,1,0:T(8,128)S(1)} %get-tuple-element.57), channel_id=1, source_target_pairs={{0,16},{16,0},{1,17},{17,1},{2,18},{18,2},{3,19},{19,3},{4,20},{20... | collective-permute-start | bytes 786440 | tf_op jit(solution)/shard_map/ppermute | solution.py:354
  279.3 15.5 %all-to-all-start.13 = ((f32[16,32,128]{2,1,0:T(8,128)}), f32[16,32,128]{2,1,0:T(8,128)S(1)}, u32[]{:S(2)}, u32[]{:S(2)}) async-start(f32[16,32,128]{2,1,0:T(8,128)} %broadcast_in_dim.55), calls=%async_computation.13 | async-start | bytes 524288 | tf_op jit(solution)/shard_map/all_to_all | solution.py:348
  313.3 9.9 %all-to-all-start.14 = ((f32[4,144,128]{2,1,0:T(8,128)}), f32[4,144,128]{2,1,0:T(8,128)S(1)}, u32[]{:S(2)}, u32[]{:S(2)}) async-start(f32[4,144,128]{2,1,0:T(8,128)} %get-tuple-element.67), calls=%async_computation.14 | async-start | bytes 589824 | tf_op jit(solution)/shard_map/all_to_all | solution.py:348
  316.8 6.5 %collective-permute-start.3 = (f32[16,32,128]{2,1,0:T(8,128)S(1)}, f32[16,32,128]{2,1,0:T(8,128)S(1)}, u32[]{:S(2)}, u32[]{:S(2)}) collective-permute-start(f32[16,32,128]{2,1,0:T(8,128)S(1)} %get-tuple-element.66), channel_id=1, source_target_pairs={{0,16},{16,0},{1,17},{17,1},{2,18},{18,2},{3,19},{19,3},{4,20},{20... | collective-permute-start | bytes 786440 | tf_op jit(solution)/shard_map/ppermute | solution.py:354
  365.2 15.6 %all-to-all-start.17 = ((f32[16,32,128]{2,1,0:T(8,128)}), f32[16,32,128]{2,1,0:T(8,128)S(1)}, u32[]{:S(2)}, u32[]{:S(2)}) async-start(f32[16,32,128]{2,1,0:T(8,128)} %broadcast_in_dim.59), calls=%async_computation.17 | async-start | bytes 524288 | tf_op jit(solution)/shard_map/all_to_all | solution.py:348
  399.0 9.9 %all-to-all-start.18 = ((f32[4,144,128]{2,1,0:T(8,128)}), f32[4,144,128]{2,1,0:T(8,128)S(1)}, u32[]{:S(2)}, u32[]{:S(2)}) async-start(f32[4,144,128]{2,1,0:T(8,128)} %get-tuple-element.76), calls=%async_computation.18 | async-start | bytes 589824 | tf_op jit(solution)/shard_map/all_to_all | solution.py:348
  402.5 6.4 %collective-permute-start.4 = (f32[16,32,128]{2,1,0:T(8,128)S(1)}, f32[16,32,128]{2,1,0:T(8,128)S(1)}, u32[]{:S(2)}, u32[]{:S(2)}) collective-permute-start(f32[16,32,128]{2,1,0:T(8,128)S(1)} %get-tuple-element.75), channel_id=1, source_target_pairs={{0,16},{16,0},{1,17},{17,1},{2,18},{18,2},{3,19},{19,3},{4,20},{20... | collective-permute-start | bytes 786440 | tf_op jit(solution)/shard_map/ppermute | solution.py:354
  443.5 7.5 %all-to-all-start.21 = ((f32[4,16,128]{2,1,0:T(8,128)}), f32[4,16,128]{2,1,0:T(8,128)S(1)}, u32[]{:S(2)}, u32[]{:S(2)}) async-start(f32[4,16,128]{2,1,0:T(8,128)} %broadcast_in_dim.62), calls=%async_computation.21 | async-start | bytes 65536 | tf_op jit(solution)/shard_map/all_to_all | solution.py:348

commit v3 on v2

--- a/solution.py
+++ b/solution.py
@@ -12,7 +12,7 @@
 HALF = 64
 VEC = 64
 GROUP = 8
-PIECES = 4
+PIECES = 2
 GIVEN = (1, 3, 4, 4)
 STORED = (3, 4, 4, 0)
 ITERS = 4
@@ -292,7 +292,9 @@
         trial = jnp.where(mask, trials[at], 0.0)
         known = jnp.where(mask, knowns[at], 0.0)
         gram = dot(trial, trial, NT)
-        projected = dot(trial, known, NT) - STEP * dot(known, fresh[at], NT)
+        projected = dot(
+            jnp.concatenate([trial, known], axis=1), jnp.concatenate([known, -STEP * fresh[at]], axis=1), NT
+        )
         return gram, projected
 
     emit_products(

time: 463 us -> 462 us (level)
  no operation moved by 1% of the time
where the time goes in v3:
time: 462 us; the launch traced here: 460 us
  blocking collectives  274 us (59%)
  starting transfers between devices  82.2 us (18%)
  waiting for transfers between devices  51.3 us (11%)
  Pallas kernels  43.1 us (9%)
  local copies, waits for them, and re-layouts  7.37 us (2%)
    all_to_all x9, blocking collectives, exchange(): return lax.all_to_all(blocks, axes, 0, 0, tiled=True)  170 us
    all_to_all x13, starting transfers between devices, exchange(): return lax.all_to_all(blocks, axes, 0, 0, tiled=True)  68.8 us
    all_to_all x13, waiting for transfers between devices, exchange(): return lax.all_to_all(blocks, axes, 0, 0, tiled=True)  51.3 us
    all_gather x4, blocking collectives, apply_and_gather(): lax.all_gather(jnp.concatenate([blocks.reshape(n_direct, TILE), sums], ax...  46.8 us
    all_gather x4, blocking collectives, apply_and_gather(): lax.all_gather(jnp.concatenate([from_chips, sums], axis=0), 'core', axis=0)  37.9 us
    pallas_call x4, Pallas kernels, per_device(): pl.pallas_call(functools.partial(middle_kernel, step, n_row, n_col), out_...  35.5 us
    ppermute x5, starting transfers between devices, reduce_row_and_y(): both_cores = keep + lax.ppermute(give, 'core', [(0, 1), (1, 0)])  13.4 us
    all_gather x1, blocking collectives, per_device(): from_col = lax.all_gather(along_z.reshape(n_direct, TILE), 'y', axis=0)  10.2 us
  transfers between devices with their start and end apart: 18, of which 9 were waited for; matrix products, arithmetic and copies ran while one was open for 0% of the time, Pallas kernels for 0%

profile of v3, /device:TPU:1, one launch (start us, length us, event | category | flops | bytes accessed | tf_op | source)
XLA Modules:
  0.0 460.2 jit_solution(15892251666072507823)
XLA Ops:
  2.1 15.6 %all-to-all-start.1 = ((f32[4,32,128]{2,1,0:T(8,128)}), f32[4,32,128]{2,1,0:T(8,128)S(1)}, u32[]{:S(2)}, u32[]{:S(2)}) async-start(f32[4,32,128]{2,1,0:T(8,128)} %broadcast_in_dim.43), calls=%async_computation.1 | async-start | bytes 131072 | tf_op jit(solution)/shard_map/all_to_all | solution.py:350
  17.7 2.4 all_gather.57
  20.1 10.1 %all-to-all-done.1 = f32[4,32,128]{2,1,0:T(8,128)S(1)} async-done(((f32[4,32,128]{2,1,0:T(8,128)}), f32[4,32,128]{2,1,0:T(8,128)S(1)}, u32[]{:S(2)}, u32[]{:S(2)}) %all-to-all-start.1) | async-done | bytes 65568 | tf_op jit(solution)/shard_map/all_to_all | solution.py:350
  31.1 5.5 %all-to-all-start = ((f32[16,64,128]{2,1,0:T(8,128)}), f32[16,64,128]{2,1,0:T(8,128)S(1)}, u32[]{:S(2)}, u32[]{:S(2)}) async-start(f32[16,64,128]{2,1,0:T(8,128)} %broadcast_in_dim.42), calls=%async_computation | async-start | bytes 1048576 | tf_op jit(solution)/shard_map/all_to_all | solution.py:350
  36.7 10.2 %all_gather.58.recv_col_ref = f32[4,128,128]{2,1,0:T(8,128)S(1)} all-gather(f32[1,128,128]{2,1,0:T(8,128)S(1)} %bitcast.81), channel_id=1, replica_groups=mesh['x'=4,'zl'=4,'core'=2,'zh'=4,'y'=4] {'y'}, dimensions={0}, use_global_device_ids=true | all-gather | bytes 327680 | tf_op jit(solution)/shard_map/all_gather | solution.py:390
  46.9 5.1 %all-to-all-done.recv_row_ref = f32[16,64,128]{2,1,0:T(8,128)S(1)} async-done(((f32[16,64,128]{2,1,0:T(8,128)}), f32[16,64,128]{2,1,0:T(8,128)S(1)}, u32[]{:S(2)}, u32[]{:S(2)}) %all-to-all-start) | async-done | bytes 524320 | tf_op jit(solution)/shard_map/all_to_all | solution.py:350
  52.6 3.7 shard_map.67
  56.4 4.2 all-to-all-start.2
  60.6 4.2 collective-permute-start
  66.4 13.5 %all_to_all.110 = f32[16,48,128]{2,1,0:T(8,128)S(1)} all-to-all(f32[16,48,128]{2,1,0:T(8,128)S(1)} %pad_maximum_fusion), channel_id=1, replica_groups=mesh['x'=4,'zl'=4,'core'=2,'zh'=4,'y'=4] {'x','zl'}, dimensions={0} | all-to-all | bytes 786432 | tf_op jit(solution)/shard_map/all_to_all | solution.py:350
  80.7 3.5 all-to-all-start.4
  84.1 13.7 %all-to-all-done.4 = f32[4,176,128]{2,1,0:T(8,128)S(1)} async-done(((f32[4,176,128]{2,1,0:T(8,128)}), f32[4,176,128]{2,1,0:T(8,128)S(1)}, u32[]{:S(2)}, u32[]{:S(2)}) %all-to-all-start.4) | async-done | bytes 360480 | tf_op jit(solution)/shard_map/all_to_all | solution.py:350
  98.7 5.9 %all-to-all-start.5 = ((f32[16,32,128]{2,1,0:T(8,128)}), f32[16,32,128]{2,1,0:T(8,128)S(1)}, u32[]{:S(2)}, u32[]{:S(2)}) async-start(f32[16,32,128]{2,1,0:T(8,128)} %broadcast_in_dim.47), calls=%async_computation.5 | async-start | bytes 524288 | tf_op jit(solution)/shard_map/all_to_all | solution.py:350
  104.6 17.6 %all-gather = f32[576,128]{1,0:T(8,128)S(1)} all-gather(f32[144,128]{1,0:T(8,128)S(1)} %pad_maximum_fusion.14), channel_id=2, replica_groups=mesh['x'=4,'zl'=4,'core'=2,'zh'=4,'y'=4] {'y'}, dimensions={0}, use_global_device_ids=true | all-gather | bytes 368640 | tf_op jit(solution)/shard_map/all_gather | solution.py:374
  122.2 9.7 %all-gather.1 = f32[1152,128]{1,0:T(8,128)S(1)} all-gather(f32[576,128]{1,0:T(8,128)S(1)} %pad_maximum_fusion.5), channel_id=3, replica_groups=mesh['x'=4,'zl'=4,'core'=2,'zh'=4,'y'=4] {'core'}, dimensions={0}, use_global_device_ids=true | all-gather | bytes 884736 | tf_op jit(solution)/shard_map/all_gather | solution.py:376
  131.9 8.4 %shard_map.68 = (f32[24,64,128]{2,1,0:T(8,128)}, f32[24,64,128]{2,1,0:T(8,128)}, f32[24,64,128]{2,1,0:T(8,128)}, f32[16,32,128]{2,1,0:T(8,128)S(1)}, f32[16,32,128]{2,1,0:T(8,128)S(1)}, /*index=5*/f32[4,144,128]{2,1,0:T(8,128)}) custom-call(s32[3]{0:T(128)S(1)} %pad_add_fusion.where_ref.refs_0_, s32[4]{0:T(128)S(1)} %bitcast.59, ...), custom_call_target="tpu_custom_call", output_to_operand_aliasing={{0}: (6, {})} | custom-call | tf_op jit(solution)/shard_map/pallas_call | solution.py:405
  140.3 3.5 all-to-all-start.6
  146.1 4.1 all-to-all-done.6
  150.4 19.5 %all_to_all.111 = f32[16,48,128]{2,1,0:T(8,128)S(1)} all-to-all(f32[16,48,128]{2,1,0:T(8,128)S(1)} %pad_maximum_fusion.1), channel_id=1, replica_groups=mesh['x'=4,'zl'=4,'core'=2,'zh'=4,'y'=4] {'x','zl'}, dimensions={0} | all-to-all | bytes 786432 | tf_op jit(solution)/shard_map/all_to_all | solution.py:350
  169.9 22.0 %all_to_all.112 = f32[4,176,128]{2,1,0:T(8,128)S(1)} all-to-all(f32[4,176,128]{2,1,0:T(8,128)S(1)} %broadcast_in_dim.49), channel_id=1, replica_groups=mesh['x'=4,'zl'=4,'core'=2,'zh'=4,'y'=4] {'zh'}, dimensions={0} | all-to-all | bytes 720896 | tf_op jit(solution)/shard_map/all_to_all | solution.py:350
  192.7 5.4 %all-to-all-start.9 = ((f32[16,32,128]{2,1,0:T(8,128)}), f32[16,32,128]{2,1,0:T(8,128)S(1)}, u32[]{:S(2)}, u32[]{:S(2)}) async-start(f32[16,32,128]{2,1,0:T(8,128)} %broadcast_in_dim.51), calls=%async_computation.9 | async-start | bytes 524288 | tf_op jit(solution)/shard_map/all_to_all | solution.py:350
  198.2 9.7 %all-gather.2 = f32[576,128]{1,0:T(8,128)S(1)} all-gather(f32[144,128]{1,0:T(8,128)S(1)} %pad_maximum_fusion.15), channel_id=4, replica_groups=mesh['x'=4,'zl'=4,'core'=2,'zh'=4,'y'=4] {'y'}, dimensions={0}, use_global_device_ids=true | all-gather | bytes 368640 | tf_op jit(solution)/shard_map/all_gather | solution.py:374
  208.0 9.8 %all-gather.3 = f32[1152,128]{1,0:T(8,128)S(1)} all-gather(f32[576,128]{1,0:T(8,128)S(1)} %pad_maximum_fusion.6), channel_id=5, replica_groups=mesh['x'=4,'zl'=4,'core'=2,'zh'=4,'y'=4] {'core'}, dimensions={0}, use_global_device_ids=true | all-gather | bytes 884736 | tf_op jit(solution)/shard_map/all_gather | solution.py:376
  217.7 9.2 %shard_map.69 = (f32[24,64,128]{2,1,0:T(8,128)}, f32[24,64,128]{2,1,0:T(8,128)}, f32[24,64,128]{2,1,0:T(8,128)}, f32[24,64,128]{2,1,0:T(8,128)}, f32[16,32,128]{...) custom-call(s32[3]{0:T(128)S(1)} %pad_add_fusion.where_ref.refs_0_, ...), custom_call_target="tpu_custom_call", output_to_operand_aliasing={{0}: (6, {}), {1}: (7, {}), {2}: (8, {})} | custom-call | tf_op jit(solution)/shard_map/pallas_call | solution.py:405
  227.0 3.5 all-to-all-start.10
  232.7 4.2 all-to-all-done.10
  237.0 19.5 %all_to_all.113 = f32[16,48,128]{2,1,0:T(8,128)S(1)} all-to-all(f32[16,48,128]{2,1,0:T(8,128)S(1)} %pad_maximum_fusion.2), channel_id=1, replica_groups=mesh['x'=4,'zl'=4,'core'=2,'zh'=4,'y'=4] {'x','zl'}, dimensions={0} | all-to-all | bytes 786432 | tf_op jit(solution)/shard_map/all_to_all | solution.py:350
  256.6 21.3 %all_to_all.114 = f32[4,176,128]{2,1,0:T(8,128)S(1)} all-to-all(f32[4,176,128]{2,1,0:T(8,128)S(1)} %broadcast_in_dim.53), channel_id=1, replica_groups=mesh['x'=4,'zl'=4,'core'=2,'zh'=4,'y'=4] {'zh'}, dimensions={0} | all-to-all | bytes 720896 | tf_op jit(solution)/shard_map/all_to_all | solution.py:350
  278.7 5.7 %all-to-all-start.13 = ((f32[16,32,128]{2,1,0:T(8,128)}), f32[16,32,128]{2,1,0:T(8,128)S(1)}, u32[]{:S(2)}, u32[]{:S(2)}) async-start(f32[16,32,128]{2,1,0:T(8,128)} %broadcast_in_dim.55), calls=%async_computation.13 | async-start | bytes 524288 | tf_op jit(solution)/shard_map/all_to_all | solution.py:350
  284.4 9.7 %all-gather.4 = f32[576,128]{1,0:T(8,128)S(1)} all-gather(f32[144,128]{1,0:T(8,128)S(1)} %pad_maximum_fusion.16), channel_id=6, replica_groups=mesh['x'=4,'zl'=4,'core'=2,'zh'=4,'y'=4] {'y'}, dimensions={0}, use_global_device_ids=true | all-gather | bytes 368640 | tf_op jit(solution)/shard_map/all_gather | solution.py:374
  294.2 9.3 %all-gather.5 = f32[1152,128]{1,0:T(8,128)S(1)} all-gather(f32[576,128]{1,0:T(8,128)S(1)} %pad_maximum_fusion.7), channel_id=7, replica_groups=mesh['x'=4,'zl'=4,'core'=2,'zh'=4,'y'=4] {'core'}, dimensions={0}, use_global_device_ids=true | all-gather | bytes 884736 | tf_op jit(solution)/shard_map/all_gather | solution.py:376
  303.5 9.1 %shard_map.70 = (f32[24,64,128]{2,1,0:T(8,128)}, f32[24,64,128]{2,1,0:T(8,128)}, f32[24,64,128]{2,1,0:T(8,128)}, f32[24,64,128]{2,1,0:T(8,128)}, f32[16,32,128]{...) custom-call(s32[3]{0:T(128)S(1)} %pad_add_fusion.where_ref.refs_0_, ...), custom_call_target="tpu_custom_call", output_to_operand_aliasing={{0}: (6, {}), {1}: (7, {}), {2}: (8, {}), {3}: (9, {})} | custom-call | tf_op jit(solution)/shard_map/pallas_call | solution.py:405
  312.6 3.5 all-to-all-start.14
  318.4 4.1 all-to-all-done.14
  322.7 19.5 %all_to_all.115 = f32[16,48,128]{2,1,0:T(8,128)S(1)} all-to-all(f32[16,48,128]{2,1,0:T(8,128)S(1)} %pad_maximum_fusion.3), channel_id=1, replica_groups=mesh['x'=4,'zl'=4,'core'=2,'zh'=4,'y'=4] {'x','zl'}, dimensions={0} | all-to-all | bytes 786432 | tf_op jit(solution)/shard_map/all_to_all | solution.py:350
  342.3 21.3 %all_to_all.116 = f32[4,176,128]{2,1,0:T(8,128)S(1)} all-to-all(f32[4,176,128]{2,1,0:T(8,128)S(1)} %broadcast_in_dim.57), channel_id=1, replica_groups=mesh['x'=4,'zl'=4,'core'=2,'zh'=4,'y'=4] {'zh'}, dimensions={0} | all-to-all | bytes 720896 | tf_op jit(solution)/shard_map/all_to_all | solution.py:350
  364.3 5.9 %all-to-all-start.17 = ((f32[16,32,128]{2,1,0:T(8,128)}), f32[16,32,128]{2,1,0:T(8,128)S(1)}, u32[]{:S(2)}, u32[]{:S(2)}) async-start(f32[16,32,128]{2,1,0:T(8,128)} %broadcast_in_dim.59), calls=%async_computation.17 | async-start | bytes 524288 | tf_op jit(solution)/shard_map/all_to_all | solution.py:350
  370.2 9.7 %all-gather.6 = f32[576,128]{1,0:T(8,128)S(1)} all-gather(f32[144,128]{1,0:T(8,128)S(1)} %pad_maximum_fusion.17), channel_id=8, replica_groups=mesh['x'=4,'zl'=4,'core'=2,'zh'=4,'y'=4] {'y'}, dimensions={0}, use_global_device_ids=true | all-gather | bytes 368640 | tf_op jit(solution)/shard_map/all_gather | solution.py:374
  380.0 9.1 %all-gather.7 = f32[1152,128]{1,0:T(8,128)S(1)} all-gather(f32[576,128]{1,0:T(8,128)S(1)} %pad_maximum_fusion.8), channel_id=9, replica_groups=mesh['x'=4,'zl'=4,'core'=2,'zh'=4,'y'=4] {'core'}, dimensions={0}, use_global_device_ids=true | all-gather | bytes 884736 | tf_op jit(solution)/shard_map/all_gather | solution.py:376
  389.2 8.7 %shard_map.71 = (f32[64,128]{1,0:T(8,128)S(1)}, f32[64,128]{1,0:T(8,128)S(1)}, f32[16,32,128]{2,1,0:T(8,128)S(1)}, f32[16,32,128]{2,1,0:T(8,128)S(1)}, f32[4,144,128]{2,1,0:T(8,128)}) custom-call(s32[3]{0:T(128)S(1)} %pad_add_fusion.where_ref.refs_0_, s32[4]{0:T(128)S(1)} %bitcast.62, s32[4]{0:T(128)S(1)} %bitcast.67, f32[4,128,128]{2,1,0:T(8,128)S(1)} %bitcast.45, ...), custom_call_target="tpu_custom_call" | custom-call | tf_op jit(solution)/shard_map/pallas_call | solution.py:405
  397.8 3.5 all-to-all-start.18
  403.6 4.2 all-to-all-done.18
  407.9 19.5 %all_to_all.117 = f32[16,48,128]{2,1,0:T(8,128)S(1)} all-to-all(f32[16,48,128]{2,1,0:T(8,128)S(1)} %pad_maximum_fusion.4), channel_id=1, replica_groups=mesh['x'=4,'zl'=4,'core'=2,'zh'=4,'y'=4] {'x','zl'}, dimensions={0} | all-to-all | bytes 786432 | tf_op jit(solution)/shard_map/all_to_all | solution.py:350
  427.4 14.2 %all_to_all.118 = f32[4,48,128]{2,1,0:T(8,128)S(1)} all-to-all(f32[4,48,128]{2,1,0:T(8,128)S(1)} %pad_maximum_fusion.9), channel_id=1, replica_groups=mesh['x'=4,'zl'=4,'core'=2,'zh'=4,'y'=4] {'zh'}, dimensions={0} | all-to-all | bytes 196608 | tf_op jit(solution)/shard_map/all_to_all | solution.py:350
  442.3 3.3 all-to-all-start.21
  445.6 4.3 all-to-all-done.21
  449.9 6.4 %all_gather.75.recv_ref = f32[2,64,128]{2,1,0:T(8,128)S(1)} all-gather(f32[1,64,128]{2,1,0:T(8,128)S(1)} %bitcast.82), channel_id=1, replica_groups=mesh['x'=4,'zl'=4,'core'=2,'zh'=4,'y'=4] {'core'}, dimensions={0}, use_global_device_ids=true | all-gather | bytes 98304 | tf_op jit(solution)/shard_map/all_gather | solution.py:384
  456.3 3.9 shard_map.72
  (102 shorter events, 19.0 us)
Async XLA Ops:
  2.1 28.1 %all-to-all-start.1 = ((f32[4,32,128]{2,1,0:T(8,128)}), f32[4,32,128]{2,1,0:T(8,128)S(1)}, u32[]{:S(2)}, u32[]{:S(2)}) async-start(f32[4,32,128]{2,1,0:T(8,128)} %broadcast_in_dim.43), calls=%async_computation.1 | async-start | bytes 131072 | tf_op jit(solution)/shard_map/all_to_all | solution.py:350
  31.1 20.9 %all-to-all-start = ((f32[16,64,128]{2,1,0:T(8,128)}), f32[16,64,128]{2,1,0:T(8,128)S(1)}, u32[]{:S(2)}, u32[]{:S(2)}) async-start(f32[16,64,128]{2,1,0:T(8,128)} %broadcast_in_dim.42), calls=%async_computation | async-start | bytes 1048576 | tf_op jit(solution)/shard_map/all_to_all | solution.py:350
  36.6 15.4 %copy-start = (f32[1,1,4,128,128]{4,3,2,1,0:T(8,128)S(1)}, f32[1,1,4,128,128]{4,3,2,1,0:T(8,128)}, u32[]{:S(2)}) copy-start(f32[1,1,4,128,128]{4,3,2,1,0:T(8,128)} %param.5) | copy-start | bytes 786436
  52.0 0.7 copy-start.1
  52.0 0.7 copy-start.2
  56.4 9.9 %all-to-all-start.2 = ((f32[4,144,128]{2,1,0:T(8,128)}), f32[4,144,128]{2,1,0:T(8,128)S(1)}, u32[]{:S(2)}, u32[]{:S(2)}) async-start(f32[4,144,128]{2,1,0:T(8,128)} %get-tuple-element.44), calls=%async_computation.2 | async-start | bytes 589824 | tf_op jit(solution)/shard_map/all_to_all | solution.py:350
  60.6 5.7 %collective-permute-start = (f32[16,32,128]{2,1,0:T(8,128)S(1)}, f32[16,32,128]{2,1,0:T(8,128)S(1)}, u32[]{:S(2)}, u32[]{:S(2)}) collective-permute-start(f32[16,32,128]{2,1,0:T(8,128)S(1)} %get-tuple-element.43), channel_id=1, source_target_pairs={{0,16},{16,0},{1,17},{17,1},{2,18},{18,2},{3,19},{19,3},{4,20},{20... | collective-permute-start | bytes 786440 | tf_op jit(solution)/shard_map/ppermute | solution.py:356
  80.7 17.2 %all-to-all-start.4 = ((f32[4,176,128]{2,1,0:T(8,128)}), f32[4,176,128]{2,1,0:T(8,128)S(1)}, u32[]{:S(2)}, u32[]{:S(2)}) async-start(f32[4,176,128]{2,1,0:T(8,128)} %broadcast_in_dim.45), calls=%async_computation.4 | async-start | bytes 720896 | tf_op jit(solution)/shard_map/all_to_all | solution.py:350
  98.7 23.5 %all-to-all-start.5 = ((f32[16,32,128]{2,1,0:T(8,128)}), f32[16,32,128]{2,1,0:T(8,128)S(1)}, u32[]{:S(2)}, u32[]{:S(2)}) async-start(f32[16,32,128]{2,1,0:T(8,128)} %broadcast_in_dim.47), calls=%async_computation.5 | async-start | bytes 524288 | tf_op jit(solution)/shard_map/all_to_all | solution.py:350
  140.3 9.9 %all-to-all-start.6 = ((f32[4,144,128]{2,1,0:T(8,128)}), f32[4,144,128]{2,1,0:T(8,128)S(1)}, u32[]{:S(2)}, u32[]{:S(2)}) async-start(f32[4,144,128]{2,1,0:T(8,128)} %get-tuple-element.50), calls=%async_computation.6 | async-start | bytes 589824 | tf_op jit(solution)/shard_map/all_to_all | solution.py:350
  143.8 6.4 %collective-permute-start.1 = (f32[16,32,128]{2,1,0:T(8,128)S(1)}, f32[16,32,128]{2,1,0:T(8,128)S(1)}, u32[]{:S(2)}, u32[]{:S(2)}) collective-permute-start(f32[16,32,128]{2,1,0:T(8,128)S(1)} %get-tuple-element.49), channel_id=1, source_target_pairs={{0,16},{16,0},{1,17},{17,1},{2,18},{18,2},{3,19},{19,3},{4,20},{20... | collective-permute-start | bytes 786440 | tf_op jit(solution)/shard_map/ppermute | solution.py:356
  192.7 15.2 %all-to-all-start.9 = ((f32[16,32,128]{2,1,0:T(8,128)}), f32[16,32,128]{2,1,0:T(8,128)S(1)}, u32[]{:S(2)}, u32[]{:S(2)}) async-start(f32[16,32,128]{2,1,0:T(8,128)} %broadcast_in_dim.51), calls=%async_computation.9 | async-start | bytes 524288 | tf_op jit(solution)/shard_map/all_to_all | solution.py:350
  227.0 9.9 %all-to-all-start.10 = ((f32[4,144,128]{2,1,0:T(8,128)}), f32[4,144,128]{2,1,0:T(8,128)S(1)}, u32[]{:S(2)}, u32[]{:S(2)}) async-start(f32[4,144,128]{2,1,0:T(8,128)} %get-tuple-element.58), calls=%async_computation.10 | async-start | bytes 589824 | tf_op jit(solution)/shard_map/all_to_all | solution.py:350
  230.4 6.5 %collective-permute-start.2 = (f32[16,32,128]{2,1,0:T(8,128)S(1)}, f32[16,32,128]{2,1,0:T(8,128)S(1)}, u32[]{:S(2)}, u32[]{:S(2)}) collective-permute-start(f32[16,32,128]{2,1,0:T(8,128)S(1)} %get-tuple-element.57), channel_id=1, source_target_pairs={{0,16},{16,0},{1,17},{17,1},{2,18},{18,2},{3,19},{19,3},{4,20},{20... | collective-permute-start | bytes 786440 | tf_op jit(solution)/shard_map/ppermute | solution.py:356
  278.7 15.5 %all-to-all-start.13 = ((f32[16,32,128]{2,1,0:T(8,128)}), f32[16,32,128]{2,1,0:T(8,128)S(1)}, u32[]{:S(2)}, u32[]{:S(2)}) async-start(f32[16,32,128]{2,1,0:T(8,128)} %broadcast_in_dim.55), calls=%async_computation.13 | async-start | bytes 524288 | tf_op jit(solution)/shard_map/all_to_all | solution.py:350
  312.6 9.9 %all-to-all-start.14 = ((f32[4,144,128]{2,1,0:T(8,128)}), f32[4,144,128]{2,1,0:T(8,128)S(1)}, u32[]{:S(2)}, u32[]{:S(2)}) async-start(f32[4,144,128]{2,1,0:T(8,128)} %get-tuple-element.67), calls=%async_computation.14 | async-start | bytes 589824 | tf_op jit(solution)/shard_map/all_to_all | solution.py:350
  316.1 6.4 %collective-permute-start.3 = (f32[16,32,128]{2,1,0:T(8,128)S(1)}, f32[16,32,128]{2,1,0:T(8,128)S(1)}, u32[]{:S(2)}, u32[]{:S(2)}) collective-permute-start(f32[16,32,128]{2,1,0:T(8,128)S(1)} %get-tuple-element.66), channel_id=1, source_target_pairs={{0,16},{16,0},{1,17},{17,1},{2,18},{18,2},{3,19},{19,3},{4,20},{20... | collective-permute-start | bytes 786440 | tf_op jit(solution)/shard_map/ppermute | solution.py:356
  364.3 15.7 %all-to-all-start.17 = ((f32[16,32,128]{2,1,0:T(8,128)}), f32[16,32,128]{2,1,0:T(8,128)S(1)}, u32[]{:S(2)}, u32[]{:S(2)}) async-start(f32[16,32,128]{2,1,0:T(8,128)} %broadcast_in_dim.59), calls=%async_computation.17 | async-start | bytes 524288 | tf_op jit(solution)/shard_map/all_to_all | solution.py:350
  397.8 9.9 %all-to-all-start.18 = ((f32[4,144,128]{2,1,0:T(8,128)}), f32[4,144,128]{2,1,0:T(8,128)S(1)}, u32[]{:S(2)}, u32[]{:S(2)}) async-start(f32[4,144,128]{2,1,0:T(8,128)} %get-tuple-element.76), calls=%async_computation.18 | async-start | bytes 589824 | tf_op jit(solution)/shard_map/all_to_all | solution.py:350
  401.3 6.5 %collective-permute-start.4 = (f32[16,32,128]{2,1,0:T(8,128)S(1)}, f32[16,32,128]{2,1,0:T(8,128)S(1)}, u32[]{:S(2)}, u32[]{:S(2)}) collective-permute-start(f32[16,32,128]{2,1,0:T(8,128)S(1)} %get-tuple-element.75), channel_id=1, source_target_pairs={{0,16},{16,0},{1,17},{17,1},{2,18},{18,2},{3,19},{19,3},{4,20},{20... | collective-permute-start | bytes 786440 | tf_op jit(solution)/shard_map/ppermute | solution.py:356
  442.3 7.5 %all-to-all-start.21 = ((f32[4,16,128]{2,1,0:T(8,128)}), f32[4,16,128]{2,1,0:T(8,128)S(1)}, u32[]{:S(2)}, u32[]{:S(2)}) async-start(f32[4,16,128]{2,1,0:T(8,128)} %broadcast_in_dim.62), calls=%async_computation.21 | async-start | bytes 65536 | tf_op jit(solution)/shard_map/all_to_all | solution.py:350
